TPU v7x, 256 devices: a whole 4x4x8 slice. The times are simulated.
256 devices in a mesh: expert: 64 (over y, z, core), blk: 4 (over x).
Axes of the slice: x: 4, y: 4, z: 8, core: 2. Of those that a mesh axis runs over, the one named last changes fastest.
Arguments:
- activations: bfloat16 [131072, 2048], P(('expert', 'blk')), may hold values from -6 to 6
- destination: int32 [16384, 1], P(('expert', 'blk')), may hold values from 0 to 63; in each aligned block of 64 rows (0 to 63, 64 to 127, ...) at most 2 rows name the same one
Outputs:
- hessian: float32 [64, 2048, 2048], P('expert', 'blk')
Inputs may be any that keep to these rules, and one draw needn't show every extreme that they name: `destination`: among the 64 blocks of one device (aligned runs of 64 entries), no expert is named more than 2 times, a bound that the blocks of some device reach; every expert is named somewhere.
All inputs are finite; a program needn't handle non-finite values.
Results may differ from a plain program's by a relative error of at most 0.0003.
Values may be sent and summed in bfloat16 or wider, within the bound.
No kernel may reach another device: no remote copies, remote signals or barrier semaphores. Data moves between devices by JAX's collectives and lax.ppermute only.
A program may use at most 128 MiB of HBM per device.

v0:
```python
import jax
import jax.numpy as jnp
from jax import lax
from jax.sharding import PartitionSpec as P


def outer_rows(left_rows, right_rows):
    return lax.dot_general(
        left_rows, right_rows, (((0,), (0,)), ((), ())), preferred_element_type=jnp.float32
    )


def on_device(activations, destination):
    targets = destination[:, 0]
    block_count = targets.shape[0]
    block_rows = activations.shape[0] // block_count
    hidden_width = activations.shape[1]
    groups = lax.axis_size("expert")
    capacity = 2 * block_count // groups
    positions = jnp.arange(block_count, dtype=jnp.int32)
    same_target = targets[:, None] == targets[None, :]
    earlier = positions[None, :] < positions[:, None]
    ranking = jnp.sum((same_target & earlier).astype(jnp.int32), axis=1)
    slot_ids = targets * capacity + ranking
    selector = (
        slot_ids[None, :] == jnp.arange(groups * capacity, dtype=jnp.int32)[:, None]
    ).astype(jnp.bfloat16)
    packed = jnp.dot(
        selector,
        activations.reshape(block_count, block_rows * hidden_width),
        preferred_element_type=jnp.float32,
    )
    packed = packed.astype(jnp.bfloat16).reshape(groups, capacity * block_rows, hidden_width)
    sent_counts = jnp.sum(
        (targets[None, :] == jnp.arange(groups, dtype=jnp.int32)[:, None]).astype(jnp.float32),
        axis=1,
    )
    sent_counts = sent_counts.astype(jnp.bfloat16).reshape(groups, 1)
    strip_index = lax.axis_index("blk")
    strip_width = hidden_width // lax.axis_size("blk")
    received, got_counts = (
        lax.all_to_all(packed, "expert", split_axis=0, concat_axis=0, tiled=True),
        lax.all_to_all(sent_counts, "expert", split_axis=0, concat_axis=0, tiled=True),
    )
    received = received.reshape(groups * capacity * block_rows, hidden_width)
    total_blocks = lax.psum(jnp.sum(got_counts.astype(jnp.float32)), "blk")
    piece = lax.all_gather(received, "blk", axis=0, tiled=True)
    strip_cols = lax.dynamic_slice_in_dim(piece, strip_index * strip_width, strip_width, 1)
    gram = outer_rows(strip_cols, piece)
    scale = 2.0 / (block_rows * total_blocks)
    return (gram * scale)[None]


def solution(mesh):
    in_specs = (P(("expert", "blk"), None), P(("expert", "blk"), None))
    out_specs = P("expert", "blk", None)
    return jax.shard_map(
        on_device, mesh=mesh, in_specs=in_specs, out_specs=out_specs, check_vma=False
    )
```

profile of v0, /device:TPU:8, one launch (start us, length us, event | category | flops | bytes accessed | tf_op | source)
XLA Modules:
  0.0 305.3 jit_solution(201722477516713855)
XLA Ops:
  6.5 0.0 all-gather.2.cloned.1.call-start
  6.5 0.9 convert_reduce_fusion.2
  7.4 0.7 multiply_add_fusion
  8.1 2.9 reshape.43
  11.0 3.2 %convolution_convert_fusion = bf16[128,16384]{1,0:T(8,128)(2,1)} fusion(bf16[64,16384]{1,0:T(8,128)(2,1)S(1)} %reshape.43, s32[64]{0:T(128)S(1)} %multiply_add_fusion), kind=kOutput, calls=%fused_computation | convolution fusion | flops 270540800 | bytes 6291712 | tf_op jit(solution)/shard_map/dot_general | solution.py:28
  14.2 7.4 %reshape.44 = bf16[64,16,2048]{2,1,0:T(8,128)(2,1)} reshape(bf16[128,16384]{1,0:T(8,128)(2,1)} %convolution_convert_fusion) | data formatting | bytes 8388608 | tf_op jit(solution)/shard_map/reshape | solution.py:33
  21.6 106.7 %all_to_all.11 = bf16[64,16,2048]{2,1,0:T(8,128)(2,1)} all-to-all(bf16[64,16,2048]{2,1,0:T(8,128)(2,1)} %reshape.44), channel_id=1, replica_groups=mesh['expert'=64,'blk'=4] {'expert'}, dimensions={0} | all-to-all | bytes 8388608 | tf_op jit(solution)/shard_map/all_to_all | solution.py:42
  128.3 0.0 copy-start
  128.3 0.0 all-gather.2.cloned.1.call-update
  128.4 0.6 copy-done
  129.0 0.1 convert_reduce_fusion.1
  129.1 0.7 copy.4
  129.8 7.5 %all-to-all-start.1 = ((bf16[64,1,1]{2,1,0:T(2,128)(2,1)}), bf16[64,1,1]{2,1,0:T(2,128)(2,1)S(1)}, u32[]{:S(2)}, u32[]{:S(2)}) async-start(bf16[64,1,1]{2,1,0:T(2,128)(2,1)} %copy.4), calls=%async_computation.1 | async-start | bytes 65536 | tf_op jit(solution)/shard_map/all_to_all | solution.py:43
  137.4 8.5 %all-to-all-done.1 = bf16[64,1,1]{2,1,0:T(2,128)(2,1)S(1)} async-done(((bf16[64,1,1]{2,1,0:T(2,128)(2,1)}), bf16[64,1,1]{2,1,0:T(2,128)(2,1)S(1)}, u32[]{:S(2)}, u32[]{:S(2)}) %all-to-all-start.1) | async-done | bytes 160 | tf_op jit(solution)/shard_map/all_to_all | solution.py:43
  145.9 0.7 convert_reduce_fusion
  146.6 11.2 %psum.7 = f32[]{:T(128)} all-reduce(f32[]{:T(128)} %convert_reduce_fusion), channel_id=1, replica_groups=mesh['expert'=64,'blk'=4] {'blk'}, use_global_device_ids=true, to_apply=%region_3.0 | all-reduce | flops 1 | bytes 8 | tf_op jit(solution)/shard_map/psum | solution.py:46
  158.5 125.1 %all-gather.2.cloned.1.call-done = bf16[4096,2048]{1,0:T(8,128)(2,1)} async-done(((bf16[1024,2048]{1,0:T(8,128)(2,1)}), bf16[4096,2048]{1,0:T(8,128)(2,1)}) %all-gather.2.cloned.1.call-update) | async-done | bytes 16777232 | tf_op jit(solution)/shard_map/all_gather | solution.py:47
  283.5 14.9 %multiply_bitcast_fusion = f32[1,512,2048]{2,1,0:T(8,128)} fusion(bf16[4096,2048]{1,0:T(8,128)(2,1)} %all-gather.2.cloned.1.call-done, s32[]{:T(128)S(6)} %select_n.3, f32[]{:T(128)S(6)} %div.3), kind=kOutput, calls=%fused_computation.1 | convolution fusion | flops 8590983168 | bytes 25165832 | tf_op jit(solution)/shard_map/dot_general | solution.py:8
Async XLA Ops:
  6.5 277.0 %all-gather.2.cloned.1.call-start = ((), (), s32[]{:S(2)}) async-start(), calls=%async_computation.2 | async-start | bytes 20971520 | tf_op jit(solution)/shard_map/all_gather | solution.py:47
  128.3 0.7 copy-start
  129.8 16.0 %all-to-all-start.1 = ((bf16[64,1,1]{2,1,0:T(2,128)(2,1)}), bf16[64,1,1]{2,1,0:T(2,128)(2,1)S(1)}, u32[]{:S(2)}, u32[]{:S(2)}) async-start(bf16[64,1,1]{2,1,0:T(2,128)(2,1)} %copy.4), calls=%async_computation.1 | async-start | bytes 65536 | tf_op jit(solution)/shard_map/all_to_all | solution.py:43
Sparse Core Ops, SparseCore 0:
  128.5 155.0 all-gather.1
where the time goes:
time: 307 us; the launch traced here: 305 us
  waiting for transfers between devices  134 us (44%)
  blocking collectives  118 us (38%)
  matrix products  18.2 us (6%)
  between operations  14.1 us (5%)
  local copies, waits for them, and re-layouts  11.7 us (4%)
  starting transfers between devices  7.52 us (2%)
    all_gather x1, waiting for transfers between devices, on_device(): piece = lax.all_gather(received, 'blk', axis=0, tiled=True)  125 us
    all_to_all x1, blocking collectives, on_device(): lax.all_to_all(packed, 'expert', split_axis=0, concat_axis=0, tiled=True)  107 us
    dot_general x1, matrix products, outer_rows(): lax.dot_general(left_rows, right_rows, (((0,), (0,)), ((), ())), preferre...  14.9 us
    psum x1, blocking collectives, on_device(): total_blocks = lax.psum(jnp.sum(got_counts.astype(jnp.float32)), 'blk')  11.2 us
    all_to_all x1, waiting for transfers between devices, on_device(): lax.all_to_all(sent_counts, 'expert', split_axis=0, concat_axis=0, tiled=...  8.51 us
    all_to_all x1, starting transfers between devices, on_device(): lax.all_to_all(sent_counts, 'expert', split_axis=0, concat_axis=0, tiled=...  7.52 us
    reshape x1, local copies, waits for them, and re-layouts, on_device(): packed.astype(jnp.bfloat16)  7.41 us
  transfers between devices with their start and end apart: 2, of which 2 were waited for; matrix products, arithmetic and copies ran while one was open for 0% of the time, Pallas kernels for 0%

commit v1 on v0

v1 whole, which is shorter than its diff:
```python
import functools

import jax
import jax.numpy as jnp
from jax import lax
from jax.experimental import pallas as pl
from jax.experimental.pallas import tpu as pltpu
from jax.sharding import PartitionSpec as P

FIRST = 384
WIRE = jnp.float16
NOTE = 16
MARK = 64.0
TOP = 8192.0


def rows_dot(left, right):
    return lax.dot_general(
        left, right, (((0,), (0,)), ((), ())), preferred_element_type=jnp.float32
    )


def write_note(out_ref, place, rows, facts_ref):
    shape = (NOTE, out_ref.shape[-1])
    row = lax.broadcasted_iota(jnp.int32, shape, 0)
    note = jnp.where(row == 0, facts_ref[1], jnp.where(row == 1, facts_ref[2], facts_ref[3]))
    out_ref[place + (pl.ds(rows, NOTE),)] = note


def first_kernel(owners_ref, facts_ref, x0_ref, out_ref):
    first = x0_ref.shape[1] // 4
    half = first // 2
    scale = facts_ref[0]
    for i in range(out_ref.shape[0]):
        column = pl.multiple_of(owners_ref[i] * first, 128)
        left = x0_ref[:, pl.ds(column, first)]
        for j in range(x0_ref.shape[1] // 512):
            block = rows_dot(left, x0_ref[:, 512 * j : 512 * (j + 1)]) * scale
            out_ref[i, 0, :half, 512 * j : 512 * (j + 1)] = block[:half]
            out_ref[i, 1, :half, 512 * j : 512 * (j + 1)] = block[half:]
        write_note(out_ref, (i, 0), half, facts_ref)
        write_note(out_ref, (i, 1), half, facts_ref)


def second_kernel(owners_ref, facts_ref, x0_ref, x1_ref, out_ref):
    first = x0_ref.shape[1] // 4
    last = x1_ref.shape[1] // 4
    scale = facts_ref[0]
    for i in range(out_ref.shape[0]):
        left0 = x0_ref[:, pl.ds(pl.multiple_of(owners_ref[i] * first, 128), first)]
        left1 = x1_ref[:, pl.ds(pl.multiple_of(owners_ref[i] * last, 128), last)]
        out_ref[i, 0, :first] = rows_dot(left0, x1_ref[...]) * scale
        corner = rows_dot(left1, x1_ref[...]) * scale
        out_ref[i, 0, first : first + last // 2] = corner[: last // 2]
        out_ref[i, 1, : last // 2] = corner[last // 2 :]
        for j in range(x0_ref.shape[1] // 512):
            row = last // 2 + last * j
            block = rows_dot(left1, x0_ref[:, 512 * j : 512 * (j + 1)]) * scale
            out_ref[i, 1, row : row + last] = block
        write_note(out_ref, (i, 0), first + last // 2, facts_ref)
        write_note(out_ref, (i, 1), first + last // 2, facts_ref)


def partial_grams(kernel, rows, wide, owners, facts, *arrays):
    count = owners.shape[0]
    shape = (count, 2, rows + NOTE, wide)
    smem = pl.BlockSpec(memory_space=pltpu.SMEM)
    vmem = pl.BlockSpec(memory_space=pltpu.VMEM)
    flops = 4 * count * rows * wide * arrays[0].shape[0]
    return pl.pallas_call(
        kernel,
        out_shape=jax.ShapeDtypeStruct(shape, jnp.float32),
        in_specs=[smem, smem] + [vmem] * len(arrays),
        out_specs=vmem,
        compiler_params=pltpu.CompilerParams(vmem_limit_bytes=40 * 1024 * 1024),
        cost_estimate=pl.CostEstimate(flops=flops, bytes_accessed=4 << 20, transcendentals=0),
    )(owners, facts, *arrays)


def note_of(got):
    rows = got.shape[0] - NOTE
    return tuple(got[rows + i : rows + i + 1].astype(jnp.float32) for i in range(3))


def fourth(value):
    return (value * value) * (value * value)


class Ring:
    def __init__(self, grams, facts, ranks):
        self.grams, self.ranks = grams, ranks
        self.coarse, self.fine, self.count = facts[1], facts[2], facts[3]
        self.unit = fourth(self.coarse * self.fine)

    def send(self, values, step):
        pairs = [(i, (i + step) % self.ranks) for i in range(self.ranks)]
        return lax.ppermute(values.astype(WIRE), "blk", pairs)

    def start(self):
        far = self.grams((2,))[0]
        self.far = self.send(far[0], 1), self.send(far[1], -1)
        self.near = self.grams((1, -1))
        self.direct = self.send(self.near[0, 1], 1), self.send(self.near[1, 0], -1)

    def merge(self, mine, got):
        coarse, fine, count = note_of(got)
        unit = fourth(coarse * fine)
        larger = jnp.maximum(unit, self.unit)
        row = lax.broadcasted_iota(jnp.int32, mine.shape, 0)
        rows = mine.shape[0] - NOTE
        both = mine * (self.unit / larger) + got.astype(jnp.float32) * (unit / larger)
        coarse = jnp.where(unit > self.unit, coarse, self.coarse)
        fine = jnp.where(unit > self.unit, fine, self.fine)
        note = jnp.where(row == rows, coarse, jnp.where(row == rows + 1, fine, self.count + count))
        return jnp.where(row < rows, both, note)

    def pass_on(self):
        self.merged = (
            self.send(self.merge(self.near[0, 0], self.far[0]), 1),
            self.send(self.merge(self.near[1, 1], self.far[1]), -1),
        )

    def total(self):
        own = self.grams((0,))[0]
        rows = own.shape[1] - NOTE
        halves = []
        for half, parts in (
            (0, (self.merged[0], self.direct[1])),
            (1, (self.direct[0], self.merged[1])),
        ):
            value = own[half, :rows] * self.unit
            for got in parts:
                coarse, fine, _ = note_of(got)
                value = value + got[:rows].astype(jnp.float32) * fourth(coarse * fine)
            halves.append(value * (1.0 / TOP))
        return halves, self.count + note_of(self.merged[0])[2] + note_of(self.direct[1])[2]


def on_device(activations, destination):
    targets = destination[:, 0]
    block_count = targets.shape[0]
    rows, width = activations.shape
    block_rows = rows // block_count
    groups = lax.axis_size("expert")
    ranks = lax.axis_size("blk")
    strip = width // ranks
    last = strip - FIRST
    capacity = 2
    slot_rows = groups * capacity * block_rows
    me = lax.axis_index("blk")

    positions = jnp.arange(block_count, dtype=jnp.int32)
    same_target = targets[:, None] == targets[None, :]
    earlier = positions[None, :] < positions[:, None]
    ranking = jnp.sum((same_target & earlier).astype(jnp.int32), axis=1)
    slots = targets * capacity + ranking
    row_slots = (
        slots[:, None] * block_rows + jnp.arange(block_rows, dtype=jnp.int32)[None, :]
    ).reshape(rows)
    chosen = row_slots[None, :] == jnp.arange(slot_rows, dtype=jnp.int32)[:, None]
    empty = 1.0 - jnp.sum(chosen.astype(jnp.float32), axis=1)
    selector = chosen.astype(jnp.bfloat16)

    def packed(start, stop, marked):
        cols = jnp.concatenate(
            [activations[:, d * strip + start : d * strip + stop] for d in range(ranks)], axis=1
        )
        placed = jnp.dot(selector, cols, preferred_element_type=jnp.float32)
        if marked:
            column = lax.broadcasted_iota(jnp.int32, placed.shape, 1)
            placed = placed + jnp.where(column == 0, MARK, 0.0) * empty[:, None]
        return placed.astype(jnp.bfloat16).reshape(groups, capacity * block_rows, cols.shape[1])

    def routed(x):
        got = lax.all_to_all(x, "expert", split_axis=0, concat_axis=0, tiled=True)
        return got.reshape(slot_rows, got.shape[2])

    def largest(x):
        return jnp.maximum(jnp.max(jnp.abs(x)).astype(jnp.float32), 1e-12)

    def facts_of(top, count):
        quarter = jnp.ceil(0.5 * jnp.log2(top) + 1e-3 + 0.25 * slot_rows.bit_length())
        coarse = jnp.clip(quarter, -14.0, 15.0)
        fine = jnp.clip(quarter - coarse, -14.0, 0.0)
        coarse, fine = jnp.exp2(coarse), jnp.exp2(fine)
        return jnp.stack([TOP / fourth(coarse * fine), coarse, fine, count])

    def owners(offsets):
        return jnp.stack([lax.rem(me + o + ranks, ranks) for o in offsets])

    x0 = routed(packed(0, FIRST, True))
    x0, later = lax.optimization_barrier((x0, packed(FIRST, strip, False)))
    x1 = routed(later)

    corner = x0[:, :128]
    is_mark = (corner > MARK / 2) & (lax.broadcasted_iota(jnp.int32, corner.shape, 1) == 0)
    empty_blocks = jnp.sum(is_mark.astype(jnp.float32)) / block_rows
    x0 = lax.dynamic_update_slice(x0, jnp.where(is_mark, jnp.zeros_like(corner), corner), (0, 0))

    top0 = largest(x0)
    facts0 = facts_of(top0, empty_blocks)
    ring0 = Ring(
        lambda offsets: partial_grams(
            first_kernel, FIRST // 2, ranks * FIRST, owners(offsets), facts0, x0
        ),
        facts0,
        ranks,
    )
    ring0.start()
    ring0.far, x1, top0 = lax.optimization_barrier((ring0.far, x1, top0))
    facts1 = facts_of(jnp.maximum(top0, largest(x1)), jnp.float32(0))
    ring1 = Ring(
        lambda offsets: partial_grams(
            second_kernel, FIRST + last // 2, ranks * last, owners(offsets), facts1, x0, x1
        ),
        facts1,
        ranks,
    )
    ring0.pass_on()
    ring1.start()
    ring1.pass_on()

    sums0, empty_blocks = ring0.total()
    hessian_scale = 2.0 / (float(ranks * slot_rows) - block_rows * empty_blocks)
    out = jnp.zeros((strip, width), jnp.float32)
    for half, piece in enumerate(sums0):
        for d in range(ranks):
            part = piece[:, d * FIRST : (d + 1) * FIRST] * hessian_scale[:, :FIRST]
            out = lax.dynamic_update_slice(out, part, (half * (FIRST // 2), d * strip))
    (upper, lower), _ = ring1.total()
    columns = jnp.concatenate([upper, lower[: last // 2]])
    cross = lower[last // 2 :].reshape(3, last, ranks * last)
    cross = jnp.concatenate([cross[0], cross[1], cross[2]], axis=1)
    for d in range(ranks):
        part = columns[:, d * last : (d + 1) * last] * hessian_scale[:, :last]
        out = lax.dynamic_update_slice(out, part, (0, d * strip + FIRST))
        part = cross[:, d * FIRST : (d + 1) * FIRST] * hessian_scale[:, :FIRST]
        out = lax.dynamic_update_slice(out, part, (FIRST, d * strip))
    return out[None]


def solution(mesh):
    in_specs = (P(("expert", "blk"), None), P(("expert", "blk"), None))
    out_specs = P("expert", "blk", None)
    return jax.shard_map(
        on_device, mesh=mesh, in_specs=in_specs, out_specs=out_specs, check_vma=False
    )
```

time: 307 us -> 203 us (0.66)
  blocking collectives: 118 us -> 0 us
  starting transfers between devices: 7.52 us -> 38.1 us
  waiting for transfers between devices: 134 us -> 115 us
  Pallas kernels: 0 us -> 15.2 us
  matrix products: 18.2 us -> 5.75 us
  other arithmetic: 2.35 us -> 14.6 us
  between operations: 14.1 us -> 2.68 us
    all_gather x1 -> x0, waiting for transfers between devices: 125 us -> none  [on_device(): piece = lax.all_gather(received, 'blk', axis=0, tiled=True)]
    all_to_all x1 -> x0, blocking collectives: 107 us -> none  [on_device(): lax.all_to_all(packed, 'expert', split_axis=0, concat_axis=0, tiled=True)]
    all_to_all x1 -> x2, waiting for transfers between devices: 8.51 us -> 69.5 us  [routed(): got = lax.all_to_all(x, 'expert', split_axis=0, concat_axis=0, tiled=True)]
    ppermute x0 -> x12, waiting for transfers between devices: none -> 45.7 us  [send(): return lax.ppermute(values.astype(WIRE), 'blk', pairs)]
    ppermute x0 -> x12, starting transfers between devices: none -> 18.6 us  [send(): return lax.ppermute(values.astype(WIRE), 'blk', pairs)]
    pallas_call x0 -> x6, Pallas kernels: none -> 15.2 us  [partial_grams(): pl.pallas_call(kernel, out_shape=jax.ShapeDtypeStruct(shape, jnp.float32)...]
    dot_general x2, matrix products: 18.2 us -> 5.75 us  [packed(): placed = jnp.dot(selector, cols, preferred_element_type=jnp.float32)]
    all_to_all x1 -> x2, starting transfers between devices: 7.52 us -> 19.5 us  [routed(): got = lax.all_to_all(x, 'expert', split_axis=0, concat_axis=0, tiled=True)]
  transfers between devices with their start and end apart: 2 -> 14, of which waited for: 2 -> 8; matrix products, arithmetic and copies ran while one was open for 0% -> 8% of each run, Pallas kernels for 0% -> 8%
where the time goes in v1:
time: 203 us; the launch traced here: 202 us
  waiting for transfers between devices  115 us (57%)
  starting transfers between devices  38.1 us (19%)
  Pallas kernels  15.2 us (7%)
  other arithmetic  14.6 us (7%)
  local copies, waits for them, and re-layouts  10.3 us (5%)
  matrix products  5.75 us (3%)
  between operations  2.68 us (1%)
    all_to_all x2, waiting for transfers between devices, routed(): got = lax.all_to_all(x, 'expert', split_axis=0, concat_axis=0, tiled=True)  69.5 us
    ppermute x12, waiting for transfers between devices, send(): return lax.ppermute(values.astype(WIRE), 'blk', pairs)  45.7 us
    all_to_all x2, starting transfers between devices, routed(): got = lax.all_to_all(x, 'expert', split_axis=0, concat_axis=0, tiled=True)  19.5 us
    ppermute x12, starting transfers between devices, send(): return lax.ppermute(values.astype(WIRE), 'blk', pairs)  18.6 us
    pallas_call x6, Pallas kernels, partial_grams(): pl.pallas_call(kernel, out_shape=jax.ShapeDtypeStruct(shape, jnp.float32)...  15.2 us
    dot_general x2, matrix products, packed(): placed = jnp.dot(selector, cols, preferred_element_type=jnp.float32)  5.75 us
    unnamed x18, local copies, waits for them, and re-layouts  5.33 us
  transfers between devices with their start and end apart: 14, of which 8 were waited for; matrix products, arithmetic and copies ran while one was open for 8% of the time, Pallas kernels for 8%

profile of v1, /device:TPU:8, one launch (start us, length us, event | category | flops | bytes accessed | tf_op | source)
XLA Modules:
  0.0 201.8 jit_solution(11558614979911163021)
XLA Ops:
  0.0 1.5 fusion.137
  2.2 4.0 %add_convert_fusion = bf16[1024,1536]{1,0:T(8,128)(2,1)} fusion(f32[1024]{0:T(1024)S(1)} %broadcast_subtract_fusion, f32[1536]{0:T(1024)S(1)} %fusion.92, bf16[512,384]{1,0:T(8,128)(2,1)S(1)} %get-tuple-element.44, bf16[512,384]{1,0:T(8,128)(2,1)S(1)} %get-tuple-element.45, bf16[512,384]{1,0:T(8,128)(2,1)S(1)} %get-tuple-element.46, ...), kind=kOutput, calls=%fused_computation | convolution fusion | flops 1622147072 | bytes 4730880 | tf_op jit(solution)/shard_map/dot_general | solution.py:168
  6.3 12.1 %all-to-all-start = ((bf16[64,16,1536]{2,1,0:T(8,128)(2,1)}), bf16[64,16,1536]{2,1,0:T(8,128)(2,1)S(1)}, u32[]{:S(2)}, u32[]{:S(2)}) async-start(bf16[64,16,1536]{2,1,0:T(8,128)(2,1)} %bitcast.198), calls=%async_computation | async-start | bytes 6291456 | tf_op jit(solution)/shard_map/all_to_all | solution.py:175
  18.5 1.1 fusion.136
  19.6 1.7 fusion.8
  21.3 69.4 %all-to-all-done = bf16[64,16,1536]{2,1,0:T(8,128)(2,1)S(1)} async-done(((bf16[64,16,1536]{2,1,0:T(8,128)(2,1)}), bf16[64,16,1536]{2,1,0:T(8,128)(2,1)S(1)}, u32[]{:S(2)}, u32[]{:S(2)}) %all-to-all-start) | async-done | bytes 3145760 | tf_op jit(solution)/shard_map/all_to_all | solution.py:175
  90.8 0.7 convert_reduce_fusion.1
  91.7 1.0 abs_reduce_fusion
  94.1 7.4 %all-to-all-start.1 = ((bf16[64,16,512]{2,1,0:T(8,128)(2,1)}), bf16[64,16,512]{2,1,0:T(8,128)(2,1)}, u32[]{:S(2)}, u32[]{:S(2)}) async-start(bf16[64,16,512]{2,1,0:T(8,128)(2,1)} %bitcast.199), calls=%async_computation.1 | async-start | bytes 2097152 | tf_op jit(solution)/shard_map/all_to_all | solution.py:175
  101.6 2.0 shard_map.30
  103.7 3.2 %shard_map.29 = f32[2,2,208,1536]{3,2,1,0:T(8,128)S(1)} custom-call(s32[2]{0:T(128)S(1)} %pad_add_fusion.owners_ref, f32[4]{0:T(128)S(1)} %pad_maximum_fusion.3.facts_ref, bf16[1024,1536]{1,0:T(8,128)(2,1)S(1)} %fusion.65.x0_ref), custom_call_target="tpu_custom_call" | custom-call | flops 2415919104 | bytes 4194304 | tf_op jit(solution)/shard_map/pallas_call | solution.py:70
  106.9 0.4 convert.19
  107.3 1.8 copy-done
  109.2 1.0 slice_bitcast_fusion.4
  110.2 1.5 collective-permute-start.4
  111.9 1.6 collective-permute-start
  113.5 1.8 collective-permute-start.1
  115.3 0.8 collective-permute-start.3
  116.1 2.0 shard_map.28
  118.0 1.5 copy-done.1
  119.5 9.2 %collective-permute-done.4 = f16[208,1536]{1,0:T(8,128)(2,1)S(1)} collective-permute-done((f16[208,1536]{1,0:T(8,128)(2,1)S(1)}, f16[208,1536]{1,0:T(8,128)(2,1)S(1)}, u32[]{:S(2)}, u32[]{:S(2)}) %collective-permute-start.4) | collective-permute-done | bytes 639008 | tf_op jit(solution)/shard_map/ppermute | solution.py:97
  128.7 13.0 %collective-permute-done = f16[208,1536]{1,0:T(8,128)(2,1)} collective-permute-done((f16[208,1536]{1,0:T(8,128)(2,1)S(1)}, f16[208,1536]{1,0:T(8,128)(2,1)}, u32[]{:S(2)}, u32[]{:S(2)}) %collective-permute-start) | collective-permute-done | bytes 639008 | tf_op jit(solution)/shard_map/ppermute | solution.py:97
  141.7 2.0 abs_reduce_fusion.1
  144.4 2.4 %shard_map.33 = f32[1,2,464,512]{3,2,1,0:T(8,128)S(1)} custom-call(s32[1]{0:T(128)} %bitcast.16.owners_ref, f32[4]{0:T(128)S(1)} %pad_maximum_fusion.4.facts_ref, bf16[1024,1536]{1,0:T(8,128)(2,1)S(1)} %fusion.65.x0_ref, bf16[1024,512]{1,0:T(8,128)(2,1)} %bitcast.19.x1_ref), custom_call_target="tpu_custom_call" | custom-call | flops 939524096 | bytes 4194304 | tf_op jit(solution)/shard_map/pallas_call | solution.py:70
  146.8 3.4 %shard_map.32 = f32[2,2,464,512]{3,2,1,0:T(8,128)S(1)} custom-call(s32[2]{0:T(128)S(1)} %pad_add_fusion.owners_ref, f32[4]{0:T(128)S(1)} %pad_maximum_fusion.4.facts_ref, bf16[1024,1536]{1,0:T(8,128)(2,1)S(1)} %fusion.65.x0_ref, bf16[1024,512]{1,0:T(8,128)(2,1)} %bitcast.19.x1_ref), custom_call_target="tpu_custom_call" | custom-call | flops 1879048192 | bytes 4194304 | tf_op jit(solution)/shard_map/pallas_call | solution.py:70
  150.7 0.3 collective-permute-start.6
  151.0 3.0 %collective-permute-start.10 = (f16[464,512]{1,0:T(8,128)(2,1)S(1)}, f16[464,512]{1,0:T(8,128)(2,1)S(1)}, u32[]{:S(2)}, u32[]{:S(2)}) collective-permute-start(f16[464,512]{1,0:T(8,128)(2,1)S(1)} %get-tuple-element.53), channel_id=1, source_target_pairs={{0,3},{1,0},{2,1},{3,2},{4,7},{5,4},{6,5},{7,6},{8,11},{9,8},{10,9... | collective-permute-start | bytes 1425416 | tf_op jit(solution)/shard_map/ppermute | solution.py:97
  154.0 0.5 convert.21
  154.7 0.4 collective-permute-start.8
  155.1 1.1 fusion.97
  156.2 2.3 %fusion.12 = (f16[208,1536]{1,0:T(8,128)(2,1)S(1)}, f16[208,1536]{1,0:T(8,128)(2,1)S(1)}) fusion(f32[2,2,208,1536]{3,2,1,0:T(8,128)S(1)} %bitcast.195, f16[208,1536]{1,0:T(8,128)(2,1)} %collective-permute-done.1, f32[1536]{0:T(1024)S(1)} %get-tuple-element.69, f32[1536]{0:T(1024)S(1)} %get-tuple-element.70, f32[1536]{0:T(1024)S(1)} %get-tuple-element.71, ...), kind=kLoop, calls=%fused_computation.21 | loop fusion | flops 5111808 | bytes 5173872 | tf_op jit(solution)/shard_map/convert_element_type | solution.py:97
  158.5 2.4 %shard_map.31 = f32[1,2,464,512]{3,2,1,0:T(8,128)S(1)} custom-call(s32[1]{0:T(128)} %bitcast.owners_ref, f32[4]{0:T(128)S(1)} %pad_maximum_fusion.4.facts_ref, bf16[1024,1536]{1,0:T(8,128)(2,1)S(1)} %fusion.65.x0_ref, bf16[1024,512]{1,0:T(8,128)(2,1)} %bitcast.19.x1_ref), custom_call_target="tpu_custom_call" | custom-call | flops 939524096 | bytes 4194304 | tf_op jit(solution)/shard_map/pallas_call | solution.py:70
  160.9 1.8 collective-permute-start.9
  162.7 2.0 collective-permute-done.6
  164.7 0.6 collective-permute-done.10
  165.3 3.7 %collective-permute-start.5 = (f16[208,1536]{1,0:T(8,128)(2,1)S(1)}, f16[208,1536]{1,0:T(8,128)(2,1)S(1)}, u32[]{:S(2)}, u32[]{:S(2)}) collective-permute-start(f16[208,1536]{1,0:T(8,128)(2,1)S(1)} %get-tuple-element.31), channel_id=1, source_target_pairs={{0,3},{1,0},{2,1},{3,2},{4,7},{5,4},{6,5},{7,6},{8,11},{9,8},{10,9... | collective-permute-start | bytes 1916936 | tf_op jit(solution)/shard_map/ppermute | solution.py:97
  169.1 0.7 fusion.30
  169.8 5.7 %collective-permute-done.8 = f16[464,512]{1,0:T(8,128)(2,1)S(1)} collective-permute-done((f16[464,512]{1,0:T(8,128)(2,1)S(1)}, f16[464,512]{1,0:T(8,128)(2,1)S(1)}, u32[]{:S(2)}, u32[]{:S(2)}) %collective-permute-start.8) | collective-permute-done | bytes 475168 | tf_op jit(solution)/shard_map/ppermute | solution.py:97
  175.5 1.0 collective-permute-start.7
  176.5 2.8 %collective-permute-start.11 = (f16[464,512]{1,0:T(8,128)(2,1)S(1)}, f16[464,512]{1,0:T(8,128)(2,1)S(1)}, u32[]{:S(2)}, u32[]{:S(2)}) collective-permute-start(f16[464,512]{1,0:T(8,128)(2,1)S(1)} %get-tuple-element.33), channel_id=1, source_target_pairs={{0,3},{1,0},{2,1},{3,2},{4,7},{5,4},{6,5},{7,6},{8,11},{9,8},{10,9... | collective-permute-start | bytes 1425416 | tf_op jit(solution)/shard_map/ppermute | solution.py:97
  179.3 10.4 %collective-permute-done.2 = f16[208,1536]{1,0:T(8,128)(2,1)S(1)} collective-permute-done((f16[208,1536]{1,0:T(8,128)(2,1)S(1)}, f16[208,1536]{1,0:T(8,128)(2,1)S(1)}, u32[]{:S(2)}, u32[]{:S(2)}) %collective-permute-start.2) | collective-permute-done | bytes 639008 | tf_op jit(solution)/shard_map/ppermute | solution.py:97
  189.7 0.9 subtract_divide_fusion
  190.8 1.7 fusion.20
  192.5 0.5 pad_bitcast_fusion
  193.2 4.8 %collective-permute-done.7 = f16[464,512]{1,0:T(8,128)(2,1)S(1)} collective-permute-done((f16[464,512]{1,0:T(8,128)(2,1)S(1)}, f16[464,512]{1,0:T(8,128)(2,1)S(1)}, u32[]{:S(2)}, u32[]{:S(2)}) %collective-permute-start.7) | collective-permute-done | bytes 475168 | tf_op jit(solution)/shard_map/ppermute | solution.py:97
  198.1 0.6 fusion.38
  199.1 2.0 copy-done.3
  201.1 0.7 fusion.82
  (74 shorter events, 2.8 us)
Async XLA Ops:
  0.0 1.5 copy-start.6
  6.3 84.5 %all-to-all-start = ((bf16[64,16,1536]{2,1,0:T(8,128)(2,1)}), bf16[64,16,1536]{2,1,0:T(8,128)(2,1)S(1)}, u32[]{:S(2)}, u32[]{:S(2)}) async-start(bf16[64,16,1536]{2,1,0:T(8,128)(2,1)} %bitcast.198), calls=%async_computation | async-start | bytes 6291456 | tf_op jit(solution)/shard_map/all_to_all | solution.py:175
  94.1 47.6 %all-to-all-start.1 = ((bf16[64,16,512]{2,1,0:T(8,128)(2,1)}), bf16[64,16,512]{2,1,0:T(8,128)(2,1)}, u32[]{:S(2)}, u32[]{:S(2)}) async-start(bf16[64,16,512]{2,1,0:T(8,128)(2,1)} %bitcast.199), calls=%async_computation.1 | async-start | bytes 2097152 | tf_op jit(solution)/shard_map/all_to_all | solution.py:175
  106.9 2.3 %copy-start = (f32[2,2,208,1536]{3,2,1,0:T(8,128)}, f32[2,2,208,1536]{3,2,1,0:T(8,128)S(1)}, u32[]{:S(2)}) copy-start(f32[2,2,208,1536]{3,2,1,0:T(8,128)S(1)} %shard_map.29) | copy-start | bytes 15335428
  110.2 18.4 %collective-permute-start.4 = (f16[208,1536]{1,0:T(8,128)(2,1)S(1)}, f16[208,1536]{1,0:T(8,128)(2,1)S(1)}, u32[]{:S(2)}, u32[]{:S(2)}) collective-permute-start(f16[208,1536]{1,0:T(8,128)(2,1)S(1)} %get-tuple-element.37), channel_id=1, source_target_pairs={{0,1},{1,2},{2,3},{3,0},{4,5},{5,6},{6,7},{7,4},{8,9},{9,10},{10,1... | collective-permute-start | bytes 1916936 | tf_op jit(solution)/shard_map/ppermute | solution.py:97
  111.9 29.7 %collective-permute-start = (f16[208,1536]{1,0:T(8,128)(2,1)S(1)}, f16[208,1536]{1,0:T(8,128)(2,1)}, u32[]{:S(2)}, u32[]{:S(2)}) collective-permute-start(f16[208,1536]{1,0:T(8,128)(2,1)S(1)} %get-tuple-element.52), channel_id=1, source_target_pairs={{0,1},{1,2},{2,3},{3,0},{4,5},{5,6},{6,7},{7,4},{8,9},{9,10},{10,1... | collective-permute-start | bytes 1916936 | tf_op jit(solution)/shard_map/ppermute | solution.py:97
  113.5 28.2 %collective-permute-start.1 = (f16[208,1536]{1,0:T(8,128)(2,1)S(1)}, f16[208,1536]{1,0:T(8,128)(2,1)}, u32[]{:S(2)}, u32[]{:S(2)}) collective-permute-start(f16[208,1536]{1,0:T(8,128)(2,1)S(1)} %get-tuple-element.51), channel_id=1, source_target_pairs={{0,3},{1,0},{2,1},{3,2},{4,7},{5,4},{6,5},{7,6},{8,11},{9,8},{10,9... | collective-permute-start | bytes 1916936 | tf_op jit(solution)/shard_map/ppermute | solution.py:97
  115.3 64.0 %collective-permute-start.3 = (f16[208,1536]{1,0:T(8,128)(2,1)}, f16[208,1536]{1,0:T(8,128)(2,1)}, u32[]{:S(2)}, u32[]{:S(2)}) collective-permute-start(f16[208,1536]{1,0:T(8,128)(2,1)} %get-tuple-element.38), channel_id=1, source_target_pairs={{0,3},{1,0},{2,1},{3,2},{4,7},{5,4},{6,5},{7,6},{8,11},{9,8},{10,9... | collective-permute-start | bytes 1916936 | tf_op jit(solution)/shard_map/ppermute | solution.py:97
  118.0 1.5 copy-start.1
  128.6 13.0 %copy-start.4 = (f16[208,1536]{1,0:T(8,128)(2,1)}, f16[208,1536]{1,0:T(8,128)(2,1)S(1)}, u32[]{:S(2)}) copy-start(f16[208,1536]{1,0:T(8,128)(2,1)S(1)} %collective-permute-done.4) | copy-start | bytes 1916932
  150.4 5.7 %slice-start = ((s8[5111808]{0:T(1024)(128)(4,1)}), s8[4194304]{0:T(1024)(128)(4,1)S(1)}, s32[]{:S(2)}) async-start(s8[5111808]{0:T(1024)(128)(4,1)} %bitcast.194), calls=%async_computation.2 | async-start | bytes 8388608
  150.7 14.1 %collective-permute-start.6 = (f16[464,512]{1,0:T(8,128)(2,1)S(1)}, f16[464,512]{1,0:T(8,128)(2,1)S(1)}, u32[]{:S(2)}, u32[]{:S(2)}) collective-permute-start(f16[464,512]{1,0:T(8,128)(2,1)S(1)} %get-tuple-element.54), channel_id=1, source_target_pairs={{0,1},{1,2},{2,3},{3,0},{4,5},{5,6},{6,7},{7,4},{8,9},{9,10},{10,1... | collective-permute-start | bytes 1425416 | tf_op jit(solution)/shard_map/ppermute | solution.py:97
  151.0 5.2 %slice-start.1 = ((s8[5111808]{0:T(1024)(128)(4,1)}), s8[917504]{0:T(1024)(128)(4,1)S(1)}, s32[]{:S(2)}) async-start(s8[5111808]{0:T(1024)(128)(4,1)} %bitcast.194), calls=%async_computation.3 | async-start | bytes 1835008
  151.0 14.3 %collective-permute-start.10 = (f16[464,512]{1,0:T(8,128)(2,1)S(1)}, f16[464,512]{1,0:T(8,128)(2,1)S(1)}, u32[]{:S(2)}, u32[]{:S(2)}) collective-permute-start(f16[464,512]{1,0:T(8,128)(2,1)S(1)} %get-tuple-element.53), channel_id=1, source_target_pairs={{0,3},{1,0},{2,1},{3,2},{4,7},{5,4},{6,5},{7,6},{8,11},{9,8},{10,9... | collective-permute-start | bytes 1425416 | tf_op jit(solution)/shard_map/ppermute | solution.py:97
  154.7 20.8 %collective-permute-start.8 = (f16[464,512]{1,0:T(8,128)(2,1)S(1)}, f16[464,512]{1,0:T(8,128)(2,1)S(1)}, u32[]{:S(2)}, u32[]{:S(2)}) collective-permute-start(f16[464,512]{1,0:T(8,128)(2,1)S(1)} %get-tuple-element.50), channel_id=1, source_target_pairs={{0,3},{1,0},{2,1},{3,2},{4,7},{5,4},{6,5},{7,6},{8,11},{9,8},{10,9... | collective-permute-start | bytes 1425416 | tf_op jit(solution)/shard_map/ppermute | solution.py:97
  160.9 29.8 %copy-start.2 = (f32[1,2,208,1536]{3,2,1,0:T(8,128)S(1)}, f32[1,2,208,1536]{3,2,1,0:T(8,128)}, u32[]{:S(2)}) copy-start(f32[1,2,208,1536]{3,2,1,0:T(8,128)} %copy-done.1) | copy-start | bytes 7667716
  160.9 29.8 %copy-start.5 = (f16[208,1536]{1,0:T(8,128)(2,1)S(1)}, f16[208,1536]{1,0:T(8,128)(2,1)}, u32[]{:S(2)}) copy-start(f16[208,1536]{1,0:T(8,128)(2,1)} %copy-done.4) | copy-start | bytes 1916932
  160.9 15.5 %collective-permute-start.9 = (f16[464,512]{1,0:T(8,128)(2,1)S(1)}, f16[464,512]{1,0:T(8,128)(2,1)S(1)}, u32[]{:S(2)}, u32[]{:S(2)}) collective-permute-start(f16[464,512]{1,0:T(8,128)(2,1)S(1)} %get-tuple-element.49), channel_id=1, source_target_pairs={{0,1},{1,2},{2,3},{3,0},{4,5},{5,6},{6,7},{7,4},{8,9},{9,10},{10,1... | collective-permute-start | bytes 1425416 | tf_op jit(solution)/shard_map/ppermute | solution.py:97
  164.7 25.0 %collective-permute-start.2 = (f16[208,1536]{1,0:T(8,128)(2,1)S(1)}, f16[208,1536]{1,0:T(8,128)(2,1)S(1)}, u32[]{:S(2)}, u32[]{:S(2)}) collective-permute-start(f16[208,1536]{1,0:T(8,128)(2,1)S(1)} %get-tuple-element.32), channel_id=1, source_target_pairs={{0,1},{1,2},{2,3},{3,0},{4,5},{5,6},{6,7},{7,4},{8,9},{9,10},{10,1... | collective-permute-start | bytes 1916936 | tf_op jit(solution)/shard_map/ppermute | solution.py:97
  165.3 25.4 %collective-permute-start.5 = (f16[208,1536]{1,0:T(8,128)(2,1)S(1)}, f16[208,1536]{1,0:T(8,128)(2,1)S(1)}, u32[]{:S(2)}, u32[]{:S(2)}) collective-permute-start(f16[208,1536]{1,0:T(8,128)(2,1)S(1)} %get-tuple-element.31), channel_id=1, source_target_pairs={{0,3},{1,0},{2,1},{3,2},{4,7},{5,4},{6,5},{7,6},{8,11},{9,8},{10,9... | collective-permute-start | bytes 1916936 | tf_op jit(solution)/shard_map/ppermute | solution.py:97
  175.5 22.6 %collective-permute-start.7 = (f16[464,512]{1,0:T(8,128)(2,1)S(1)}, f16[464,512]{1,0:T(8,128)(2,1)S(1)}, u32[]{:S(2)}, u32[]{:S(2)}) collective-permute-start(f16[464,512]{1,0:T(8,128)(2,1)S(1)} %get-tuple-element.34), channel_id=1, source_target_pairs={{0,1},{1,2},{2,3},{3,0},{4,5},{5,6},{6,7},{7,4},{8,9},{9,10},{10,1... | collective-permute-start | bytes 1425416 | tf_op jit(solution)/shard_map/ppermute | solution.py:97
  176.5 21.6 %collective-permute-start.11 = (f16[464,512]{1,0:T(8,128)(2,1)S(1)}, f16[464,512]{1,0:T(8,128)(2,1)S(1)}, u32[]{:S(2)}, u32[]{:S(2)}) collective-permute-start(f16[464,512]{1,0:T(8,128)(2,1)S(1)} %get-tuple-element.33), channel_id=1, source_target_pairs={{0,3},{1,0},{2,1},{3,2},{4,7},{5,4},{6,5},{7,6},{8,11},{9,8},{10,9... | collective-permute-start | bytes 1425416 | tf_op jit(solution)/shard_map/ppermute | solution.py:97
  199.1 2.0 copy-start.3

commit v2 on v0

v2 whole, which is shorter than its diff:
```python
import functools
import math

import jax
import jax.numpy as jnp
from jax import lax
from jax.experimental import pallas as pl
from jax.experimental.pallas import tpu as pltpu
from jax.sharding import PartitionSpec as P

FIRST = 384
WIRE = jnp.float16
NOTE = 16
MARK = 64.0
TOP = 8192.0


def rows_dot(left, right):
    return lax.dot_general(
        left, right, (((0,), (0,)), ((), ())), preferred_element_type=jnp.float32
    )


def top_of(x_ref):
    tops = [
        jnp.max(jnp.abs(x_ref[:, 512 * j : 512 * (j + 1)]), axis=0, keepdims=True)
        for j in range(x_ref.shape[1] // 512)
    ]
    top = tops[0]
    for other in tops[1:]:
        top = jnp.maximum(top, other)
    return jnp.maximum(jnp.max(top.astype(jnp.float32), axis=1, keepdims=True), 1e-12)


def write_facts(facts_ref, top, rows, count):
    quarter = jnp.ceil((0.5 / math.log(2.0)) * jnp.log(top) + 1e-3 + 0.25 * rows.bit_length())
    coarse = jnp.clip(quarter, -14.0, 15.0)
    fine = jnp.clip(quarter - coarse, -14.0, 0.0)
    row = lax.broadcasted_iota(jnp.int32, facts_ref.shape, 0)
    unit = jnp.where(row == 1, jnp.exp2(coarse), jnp.exp2(fine))
    facts_ref[...] = jnp.where(row == 0, top, jnp.where(row < 3, unit, count))


def scale_and_notes(facts_ref, *out_refs):
    coarse, fine, count = facts_ref[1:2, :1], facts_ref[2:3, :1], facts_ref[3:4, :1]
    for ref in out_refs:
        row = lax.broadcasted_iota(jnp.int32, (NOTE, ref.shape[1]), 0)
        note = jnp.where(row == 0, coarse, jnp.where(row == 1, fine, count))
        ref[ref.shape[0] - NOTE :, :] = note
    return TOP / fourth(coarse * fine)


def first_body(owners_ref, facts_ref, x0_ref, upper_ref, lower_ref):
    first = x0_ref.shape[1] // 4
    half = first // 2
    scale = scale_and_notes(facts_ref, upper_ref, lower_ref)
    for h, ref in enumerate((upper_ref, lower_ref)):
        left = x0_ref[:, pl.ds(pl.multiple_of(owners_ref[h] * first, 128), first)]
        left = left[:, h * half : (h + 1) * half]
        for j in range(x0_ref.shape[1] // 512):
            block = rows_dot(left, x0_ref[:, 512 * j : 512 * (j + 1)])
            ref[:half, 512 * j : 512 * (j + 1)] = block * scale


def second_body(owners_ref, facts_ref, x0_ref, x1_ref, upper_ref, lower_ref):
    first = x0_ref.shape[1] // 4
    last = x1_ref.shape[1] // 4
    half = last // 2
    scale = scale_and_notes(facts_ref, upper_ref, lower_ref)
    left0 = x0_ref[:, pl.ds(pl.multiple_of(owners_ref[0] * first, 128), first)]
    left1 = x1_ref[:, pl.ds(pl.multiple_of(owners_ref[0] * last, 128), last)]
    upper_ref[:first] = rows_dot(left0, x1_ref[...]) * scale
    upper_ref[first : first + half] = rows_dot(left1, x1_ref[...])[:half] * scale
    left1 = x1_ref[:, pl.ds(pl.multiple_of(owners_ref[1] * last, 128), last)]
    lower_ref[:half] = rows_dot(left1, x1_ref[...])[half:] * scale
    for j in range(x0_ref.shape[1] // 512):
        block = rows_dot(left1, x0_ref[:, 512 * j : 512 * (j + 1)])
        lower_ref[half + last * j : half + last * (j + 1)] = block * scale


def first_far(owners_ref, corner_ref, x0_ref, upper_ref, lower_ref, facts_ref):
    marks = jnp.where(corner_ref[:, :1].astype(jnp.float32) > MARK / 2, 1.0 / 8.0, 0.0)
    count = jnp.sum(marks, axis=0, keepdims=True)
    write_facts(facts_ref, top_of(x0_ref), x0_ref.shape[0], count)
    first_body(owners_ref, facts_ref, x0_ref, upper_ref, lower_ref)


def second_far(owners_ref, before_ref, x0_ref, x1_ref, upper_ref, lower_ref, facts_ref):
    top = jnp.maximum(before_ref[:1, :1], top_of(x1_ref))
    write_facts(facts_ref, top, x0_ref.shape[0], jnp.zeros_like(top))
    second_body(owners_ref, facts_ref, x0_ref, x1_ref, upper_ref, lower_ref)


def partial_grams(kernel, rows, wide, owners, *arrays, facts=False):
    smem = pl.BlockSpec(memory_space=pltpu.SMEM)
    vmem = pl.BlockSpec(memory_space=pltpu.VMEM)
    shapes = [jax.ShapeDtypeStruct((rows + NOTE, wide), jnp.float32)] * 2
    shapes += [jax.ShapeDtypeStruct((8, 128), jnp.float32)] * facts
    return pl.pallas_call(
        kernel,
        out_shape=shapes,
        in_specs=[smem] + [vmem] * len(arrays),
        out_specs=[vmem] * len(shapes),
        compiler_params=pltpu.CompilerParams(vmem_limit_bytes=40 * 1024 * 1024),
        cost_estimate=pl.CostEstimate(flops=0, bytes_accessed=0, transcendentals=0),
    )(owners, *arrays)


def pack_kernel(marked, start, slots_ref, activations_ref, out_ref, rows_ref, placed_ref, in_sem, out_sem):
    strip = activations_ref.shape[1] // 4
    wide = out_ref.shape[1] // 4
    fetches = [
        pltpu.make_async_copy(
            activations_ref.at[:, d * strip + start : d * strip + start + wide],
            rows_ref.at[d],
            in_sem.at[d],
        )
        for d in range(4)
    ]
    for fetch in fetches:
        fetch.start()
    shape = (out_ref.shape[0], slots_ref.shape[1])
    chosen = slots_ref[...] == lax.broadcasted_iota(jnp.int32, shape, 0)
    selector = jnp.where(chosen, 1.0, 0.0).astype(jnp.bfloat16)
    stores = []
    for d in range(4):
        fetches[d].wait()
        placed = jnp.dot(selector, rows_ref[d], preferred_element_type=jnp.float32)
        if marked and d == 0:
            used = jnp.sum(jnp.where(chosen, 1.0, 0.0), axis=1, keepdims=True)
            column = lax.broadcasted_iota(jnp.int32, placed.shape, 1)
            placed = placed + jnp.where(column == 0, MARK * (1.0 - used), 0.0)
        placed_ref[d] = placed.astype(jnp.bfloat16)
        store = pltpu.make_async_copy(
            placed_ref.at[d], out_ref.at[:, d * wide : (d + 1) * wide], out_sem.at[d]
        )
        store.start()
        stores.append(store)
    for store in stores:
        store.wait()


def pack(activations, slots, rows, start, wide, marked):
    hbm = pl.BlockSpec(memory_space=pltpu.HBM)
    return pl.pallas_call(
        functools.partial(pack_kernel, marked, start),
        out_shape=jax.ShapeDtypeStruct((rows, 4 * wide), jnp.bfloat16),
        in_specs=[pl.BlockSpec(memory_space=pltpu.VMEM), hbm],
        out_specs=hbm,
        scratch_shapes=[
            pltpu.VMEM((4, activations.shape[0], wide), jnp.bfloat16),
            pltpu.VMEM((4, rows, wide), jnp.bfloat16),
            pltpu.SemaphoreType.DMA((4,)),
            pltpu.SemaphoreType.DMA((4,)),
        ],
        compiler_params=pltpu.CompilerParams(vmem_limit_bytes=60 * 1024 * 1024),
    )(slots, activations)


def copies(pieces, sem):
    started = []
    for i, (source, target) in enumerate(pieces):
        copy = pltpu.make_async_copy(source, target, sem.at[i])
        copy.start()
        started.append(copy)
    for copy in started:
        copy.wait()


def place_first(upper_ref, lower_ref, out_ref, sem):
    half, first = upper_ref.shape[0], upper_ref.shape[1] // 4
    strip = out_ref.shape[1] // 4
    copies(
        [
            (
                ref.at[:, d * first : (d + 1) * first],
                out_ref.at[h * half : (h + 1) * half, d * strip : d * strip + first],
            )
            for h, ref in enumerate((upper_ref, lower_ref))
            for d in range(4)
        ],
        sem,
    )


def place_second(upper_ref, lower_ref, before_ref, out_ref, sem):
    rows, last = upper_ref.shape[0], upper_ref.shape[1] // 4
    strip = out_ref.shape[1] // 4
    first, half = strip - last, last // 2
    pieces = []
    for d in range(4):
        column = slice(d * strip + first, (d + 1) * strip)
        pieces.append((upper_ref.at[:, d * last : (d + 1) * last], out_ref.at[:rows, column]))
        pieces.append((lower_ref.at[:half, d * last : (d + 1) * last], out_ref.at[rows:, column]))
        for j in range(4 * first // 512):
            left, right = max(d * first, 512 * j), min((d + 1) * first, 512 * (j + 1))
            if left < right:
                row = half + last * j
                source = lower_ref.at[row : row + last, left - 512 * j : right - 512 * j]
                column = d * strip - d * first
                pieces.append((source, out_ref.at[first:, left + column : right + column]))
    copies(pieces, sem)


def place(kernel, shape, upper, lower, *before):
    hbm, vmem = pl.BlockSpec(memory_space=pltpu.HBM), pl.BlockSpec(memory_space=pltpu.VMEM)
    return pl.pallas_call(
        kernel,
        out_shape=jax.ShapeDtypeStruct(shape, jnp.float32),
        in_specs=[vmem, vmem] + [hbm] * len(before),
        out_specs=hbm,
        input_output_aliases={2: 0} if before else {},
        scratch_shapes=[pltpu.SemaphoreType.DMA((16,))],
        compiler_params=pltpu.CompilerParams(vmem_limit_bytes=24 * 1024 * 1024),
    )(upper, lower, *before)


def fourth(value):
    return (value * value) * (value * value)


def note_of(got):
    rows = got.shape[0] - NOTE
    return tuple(got[rows + i : rows + i + 1].astype(jnp.float32) for i in range(3))


class Ring:
    def __init__(self, far, grams, ranks):
        self.ranks = ranks
        upper, lower, facts = far()
        self.far = self.send(upper, 1), self.send(lower, -1)
        behind, ahead = grams(facts, -1, 1)
        self.direct = self.send(ahead, 1), self.send(behind, -1)
        self.facts = facts
        far, facts = lax.optimization_barrier((self.far, facts))
        ahead, behind = grams(facts, 1, -1)
        merged = self.merge(ahead, far[0]).astype(WIRE), self.merge(behind, far[1]).astype(WIRE)
        self.direct, merged = lax.optimization_barrier((self.direct, merged))
        self.merged = self.send(merged[0], 1), self.send(merged[1], -1)
        self.own = grams(facts, 0, 0)

    def send(self, values, step):
        pairs = [(i, (i + step) % self.ranks) for i in range(self.ranks)]
        return lax.ppermute(values.astype(WIRE), "blk", pairs)

    def merge(self, mine, got):
        got_coarse, got_fine, got_count = note_of(got)
        coarse, fine, count = note_of(mine)
        got_unit, unit = fourth(got_coarse * got_fine), fourth(coarse * fine)
        larger = jnp.maximum(unit, got_unit)
        row = lax.broadcasted_iota(jnp.int32, mine.shape, 0)
        rows = mine.shape[0] - NOTE
        both = mine * (unit / larger) + got.astype(jnp.float32) * (got_unit / larger)
        coarse = jnp.where(got_unit > unit, got_coarse, coarse)
        fine = jnp.where(got_unit > unit, got_fine, fine)
        note = jnp.where(row == rows, coarse, jnp.where(row == rows + 1, fine, count + got_count))
        return jnp.where(row < rows, both, note)

    def total(self):
        own = self.own
        rows = own[0].shape[0] - NOTE
        halves = []
        for mine, parts in (
            (own[0], (self.merged[0], self.direct[1])),
            (own[1], (self.direct[0], self.merged[1])),
        ):
            value = 0.0
            count = 0.0
            for got in (mine,) + parts:
                coarse, fine, more = note_of(got)
                value = value + got[:rows].astype(jnp.float32) * fourth(coarse * fine)
                count = count + more
            halves.append(value * (1.0 / TOP))
        return halves, count


def on_device(activations, destination):
    targets = destination[:, 0]
    block_count = targets.shape[0]
    rows, width = activations.shape
    block_rows = rows // block_count
    groups = lax.axis_size("expert")
    ranks = lax.axis_size("blk")
    strip = width // ranks
    last = strip - FIRST
    capacity = 2
    slot_rows = groups * capacity * block_rows
    me = lax.axis_index("blk")

    positions = jnp.arange(block_count, dtype=jnp.int32)
    same_target = targets[:, None] == targets[None, :]
    earlier = positions[None, :] < positions[:, None]
    ranking = jnp.sum((same_target & earlier).astype(jnp.int32), axis=1)
    slots = targets * capacity + ranking
    row_slots = (
        slots[:, None] * block_rows + jnp.arange(block_rows, dtype=jnp.int32)[None, :]
    ).reshape(1, rows)

    def packed(start, stop, marked):
        placed = pack(activations, row_slots, slot_rows, start, stop - start, marked)
        return placed.reshape(groups, capacity * block_rows, placed.shape[1])

    def routed(x):
        got = lax.all_to_all(x, "expert", split_axis=0, concat_axis=0, tiled=True)
        return got.reshape(slot_rows, got.shape[2])

    def owners(offsets):
        return jnp.stack([lax.rem(me + o + ranks, ranks) for o in offsets])

    x0 = routed(packed(0, FIRST, True))
    x0, later = lax.optimization_barrier((x0, packed(FIRST, strip, False)))
    x1 = routed(later)

    corner = x0[:, :128]
    is_mark = (corner > MARK / 2) & (lax.broadcasted_iota(jnp.int32, corner.shape, 1) == 0)
    x0 = lax.dynamic_update_slice(x0, jnp.where(is_mark, jnp.zeros_like(corner), corner), (0, 0))

    def owners(offsets):
        return jnp.stack([lax.rem(me + o + ranks, ranks) for o in offsets])

    x0 = routed(packed(0, FIRST, True))
    x0, later = lax.optimization_barrier((x0, packed(FIRST, strip, False)))
    x1 = routed(later)

    corner = x0[:, :128]
    is_mark = (corner > MARK / 2) & (lax.broadcasted_iota(jnp.int32, corner.shape, 1) == 0)
    empty_blocks = jnp.sum(is_mark.astype(jnp.float32)) / block_rows
    x0 = lax.dynamic_update_slice(x0, jnp.where(is_mark, jnp.zeros_like(corner), corner), (0, 0))

    half0, half1 = FIRST // 2, FIRST + last // 2
    ring0 = Ring(
        lambda: partial_grams(
            first_far, half0, ranks * FIRST, owners((2, 2)), corner, x0, facts=True
        ),
        lambda facts, *offsets: partial_grams(
            first_body, half0, ranks * FIRST, owners(offsets), facts, x0
        ),
        ranks,
    )
    ring0.merged, x1 = lax.optimization_barrier((ring0.merged, x1))
    ring1 = Ring(
        lambda: partial_grams(
            second_far, half1, ranks * last, owners((2, 2)), ring0.facts, x0, x1, facts=True
        ),
        lambda facts, *offsets: partial_grams(
            second_body, half1, ranks * last, owners(offsets), facts, x0, x1
        ),
        ranks,
    )

    ring0.merged, _ = lax.optimization_barrier((ring0.merged, ring1.facts))
    sums0, empty_blocks = ring0.total()
    hessian_scale = 2.0 / (float(ranks * slot_rows) - block_rows * empty_blocks)
    shape = (strip, width)
    out = place(place_first, shape, *[half * hessian_scale for half in sums0])
    sums1, _ = ring1.total()
    hessian_scale = hessian_scale[:, : ranks * last]
    out = place(place_second, shape, *[half * hessian_scale for half in sums1], out)
    return out[None]


def solution(mesh):
    in_specs = (P(("expert", "blk"), None), P(("expert", "blk"), None))
    out_specs = P("expert", "blk", None)
    return jax.shard_map(
        on_device, mesh=mesh, in_specs=in_specs, out_specs=out_specs, check_vma=False
    )
```

time: 307 us -> 193 us (0.63)
  blocking collectives: 118 us -> 0 us
  waiting for transfers between devices: 134 us -> 100 us
  Pallas kernels: 0 us -> 32.6 us
  starting transfers between devices: 7.52 us -> 39.7 us
  matrix products: 18.2 us -> 0 us
  between operations: 14.1 us -> 0.56 us
  other arithmetic: 2.35 us -> 15.6 us
  local copies, waits for them, and re-layouts: 11.7 us -> 2.79 us
    all_gather x1 -> x0, waiting for transfers between devices: 125 us -> none  [on_device(): piece = lax.all_gather(received, 'blk', axis=0, tiled=True)]
    all_to_all x1 -> x0, blocking collectives: 107 us -> none  [on_device(): lax.all_to_all(packed, 'expert', split_axis=0, concat_axis=0, tiled=True)]
    all_to_all x1 -> x2, waiting for transfers between devices: 8.51 us -> 67.1 us  [routed(): got = lax.all_to_all(x, 'expert', split_axis=0, concat_axis=0, tiled=True)]
    ppermute x0 -> x12, waiting for transfers between devices: none -> 33 us  [send(): return lax.ppermute(values.astype(WIRE), 'blk', pairs)]
    pallas_call x0 -> x12, Pallas kernels: none -> 32.6 us  [the longest x8 19 us: partial_grams(): pl.pallas_call(kernel, out_shape=shapes, in_specs=[smem] + [vmem] * len(a...]
    ppermute x0 -> x12, starting transfers between devices: none -> 20.2 us  [send(): return lax.ppermute(values.astype(WIRE), 'blk', pairs)]
    dot_general x2 -> x0, matrix products: 18.2 us -> none  [the longest x1 14.9 us: outer_rows(): lax.dot_general(left_rows, right_rows, (((0,), (0,)), ((), ())), preferre...]
    all_to_all x1 -> x2, starting transfers between devices: 7.52 us -> 19.5 us  [routed(): got = lax.all_to_all(x, 'expert', split_axis=0, concat_axis=0, tiled=True)]
  transfers between devices with their start and end apart: 2 -> 14, of which waited for: 2 -> 9; matrix products, arithmetic and copies ran while one was open for 0% -> 6% of each run, Pallas kernels for 0% -> 11%
where the time goes in v2:
time: 193 us; the launch traced here: 191 us
  waiting for transfers between devices  100 us (52%)
  starting transfers between devices  39.7 us (21%)
  Pallas kernels  32.6 us (17%)
  other arithmetic  15.6 us (8%)
  local copies, waits for them, and re-layouts  2.79 us (1%)
    all_to_all x2, waiting for transfers between devices, routed(): got = lax.all_to_all(x, 'expert', split_axis=0, concat_axis=0, tiled=True)  67.1 us
    ppermute x12, waiting for transfers between devices, send(): return lax.ppermute(values.astype(WIRE), 'blk', pairs)  33 us
    ppermute x12, starting transfers between devices, send(): return lax.ppermute(values.astype(WIRE), 'blk', pairs)  20.2 us
    all_to_all x2, starting transfers between devices, routed(): got = lax.all_to_all(x, 'expert', split_axis=0, concat_axis=0, tiled=True)  19.5 us
    pallas_call x8, Pallas kernels, partial_grams(): pl.pallas_call(kernel, out_shape=shapes, in_specs=[smem] + [vmem] * len(a...  19 us
    pallas_call x2, Pallas kernels, pack(): pl.pallas_call(functools.partial(pack_kernel, marked, start), out_shape=j...  10.7 us
    convert_element_type x2, other arithmetic, __init__(): self.merge(behind, far[1]).astype(WIRE)  4.06 us
  transfers between devices with their start and end apart: 14, of which 9 were waited for; matrix products, arithmetic and copies ran while one was open for 6% of the time, Pallas kernels for 11%

profile of v2, /device:TPU:8, one launch (start us, length us, event | category | flops | bytes accessed | tf_op | source)
XLA Modules:
  0.0 191.4 jit_solution(7520643770767125283)
XLA Ops:
  0.0 0.9 convert_reduce_fusion
  0.9 0.7 fusion.13
  1.7 0.7 add.132.slots_ref
  2.3 5.5 %shard_map.28 = bf16[1024,1536]{1,0:T(8,128)(2,1)} custom-call(s32[1,512]{1,0:T(1,128)} %add.132.slots_ref, bf16[512,2048]{1,0:T(8,128)(2,1)} %activations_ref.3), custom_call_target="tpu_custom_call" | custom-call | tf_op jit(solution)/shard_map/pallas_call | solution.py:145
  7.8 12.1 %all-to-all-start = ((bf16[64,16,1536]{2,1,0:T(8,128)(2,1)}), bf16[64,16,1536]{2,1,0:T(8,128)(2,1)S(1)}, u32[]{:S(2)}, u32[]{:S(2)}) async-start(bf16[64,16,1536]{2,1,0:T(8,128)(2,1)} %bitcast.36), calls=%async_computation | async-start | bytes 6291456 | tf_op jit(solution)/shard_map/all_to_all | solution.py:304
  20.0 5.2 %shard_map.29 = bf16[1024,512]{1,0:T(8,128)(2,1)} custom-call(s32[1,512]{1,0:T(1,128)} %add.132.slots_ref, bf16[512,2048]{1,0:T(8,128)(2,1)} %activations_ref.3), custom_call_target="tpu_custom_call" | custom-call | tf_op jit(solution)/shard_map/pallas_call | solution.py:145
  25.3 67.1 %all-to-all-done = bf16[64,16,1536]{2,1,0:T(8,128)(2,1)S(1)} async-done(((bf16[64,16,1536]{2,1,0:T(8,128)(2,1)}), bf16[64,16,1536]{2,1,0:T(8,128)(2,1)S(1)}, u32[]{:S(2)}, u32[]{:S(2)}) %all-to-all-start) | async-done | bytes 3145760 | tf_op jit(solution)/shard_map/all_to_all | solution.py:304
  92.6 2.6 %shard_map.30 = (f32[208,1536]{1,0:T(8,128)S(1)}, f32[208,1536]{1,0:T(8,128)S(1)}, f32[8,128]{1,0:T(8,128)S(1)}) custom-call(s32[2]{0:T(128)S(1)} %pad_add_fusion.1.owners_ref, bf16[1024,128]{1,0:T(8,128)(2,1)S(1)} %get-tuple-element.102.corner_ref, bf16[1024,1536]{1,0:T(8,128)(2,1)S(1)} %get-tuple-element.101.x0_ref), custom_call_target="tpu_custom_call" | custom-call | tf_op jit(solution)/shard_map/pallas_call | solution.py:99
  95.2 0.9 convert_element_type.168
  96.1 1.5 collective-permute-start.2
  97.6 0.9 convert_element_type.169
  98.5 1.7 collective-permute-start.3
  100.2 7.4 %all-to-all-start.1 = ((bf16[64,16,512]{2,1,0:T(8,128)(2,1)}), bf16[64,16,512]{2,1,0:T(8,128)(2,1)}, u32[]{:S(2)}, u32[]{:S(2)}) async-start(bf16[64,16,512]{2,1,0:T(8,128)(2,1)} %bitcast.37), calls=%async_computation.1 | async-start | bytes 2097152 | tf_op jit(solution)/shard_map/all_to_all | solution.py:304
  107.7 2.0 %shard_map.31 = (f32[208,1536]{1,0:T(8,128)S(1)}, f32[208,1536]{1,0:T(8,128)S(1)}) custom-call(s32[2]{0:T(128)S(1)} %get-tuple-element.122.owners_ref, f32[8,128]{1,0:T(8,128)S(1)} %get-tuple-element.50.facts_ref.before_ref, bf16[1024,1536]{1,0:T(8,128)(2,1)S(1)} %get-tuple-element.101.x0_ref), custom_call_target="tpu_custom_call" | custom-call | tf_op jit(solution)/shard_map/pallas_call | solution.py:99
  109.8 0.5 collective-permute-start
  110.4 3.1 %collective-permute-start.1 = (f16[208,1536]{1,0:T(8,128)(2,1)S(1)}, f16[208,1536]{1,0:T(8,128)(2,1)S(1)}, u32[]{:S(2)}, u32[]{:S(2)}) collective-permute-start(f16[208,1536]{1,0:T(8,128)(2,1)S(1)} %convert_element_type.167), channel_id=1, source_target_pairs={{0,3},{1,0},{2,1},{3,2},{4,7},{5,4},{6,5},{7,6},{8,11},{9,8},{10,9... | collective-permute-start | bytes 1916936 | tf_op jit(solution)/shard_map/ppermute | solution.py:244
  113.5 1.3 collective-permute-done.2
  114.8 1.3 collective-permute-done.3
  116.1 2.0 %shard_map.32 = (f32[208,1536]{1,0:T(8,128)S(1)}, f32[208,1536]{1,0:T(8,128)S(1)}) custom-call(s32[2]{0:T(128)S(1)} %get-tuple-element.123.owners_ref, f32[8,128]{1,0:T(8,128)S(1)} %get-tuple-element.50.facts_ref.before_ref, bf16[1024,1536]{1,0:T(8,128)(2,1)S(1)} %get-tuple-element.101.x0_ref), custom_call_target="tpu_custom_call" | custom-call | tf_op jit(solution)/shard_map/pallas_call | solution.py:99
  118.1 1.0 select_reduce_fusion.1
  119.0 1.0 select_reduce_fusion.3
  120.0 3.3 %select_convert_fusion = (f16[208,1536]{1,0:T(8,128)(2,1)}, f16[208,1536]{1,0:T(8,128)(2,1)}) fusion(f16[208,1536]{1,0:T(8,128)(2,1)} %collective-permute-done.3, f32[208,1536]{1,0:T(8,128)S(1)} %get-tuple-element.53, f32[1536]{0:T(1024)S(1)} %get-tuple-element.87, f32[1536]{0:T(1024)S(1)} %get-tuple-element.84, f32[1536]{0:T(1024)S(1)} %get-tuple-element.83, ...), kind=kLoop, calls=%fused_computation | loop fusion | flops 5111808 | bytes 5173872 | tf_op jit(solution)/shard_map/convert_element_type | solution.py:237
  123.4 5.1 %collective-permute-done = f16[208,1536]{1,0:T(8,128)(2,1)S(1)} collective-permute-done((f16[208,1536]{1,0:T(8,128)(2,1)S(1)}, f16[208,1536]{1,0:T(8,128)(2,1)S(1)}, u32[]{:S(2)}, u32[]{:S(2)}) %collective-permute-start) | collective-permute-done | bytes 639008 | tf_op jit(solution)/shard_map/ppermute | solution.py:244
  128.5 1.0 collective-permute-done.1
  129.5 0.8 copy-done.6
  130.3 1.5 collective-permute-start.4
  131.8 1.8 collective-permute-start.5
  133.6 2.0 %shard_map.37 = (f32[208,1536]{1,0:T(8,128)S(1)}, f32[208,1536]{1,0:T(8,128)S(1)}) custom-call(s32[2]{0:T(128)S(1)} %pad_add_fusion.owners_ref, f32[8,128]{1,0:T(8,128)S(1)} %get-tuple-element.50.facts_ref.before_ref, bf16[1024,1536]{1,0:T(8,128)(2,1)S(1)} %get-tuple-element.101.x0_ref), custom_call_target="tpu_custom_call" | custom-call | tf_op jit(solution)/shard_map/pallas_call | solution.py:99
  135.6 1.0 copy-done
  136.7 0.8 multiply_reduce_fusion.4
  137.8 10.4 %collective-permute-done.4 = f16[208,1536]{1,0:T(8,128)(2,1)} collective-permute-done((f16[208,1536]{1,0:T(8,128)(2,1)}, f16[208,1536]{1,0:T(8,128)(2,1)}, u32[]{:S(2)}, u32[]{:S(2)}) %collective-permute-start.4) | collective-permute-done | bytes 639008 | tf_op jit(solution)/shard_map/ppermute | solution.py:244
  148.2 2.7 %shard_map.33 = (f32[464,512]{1,0:T(8,128)S(1)}, f32[464,512]{1,0:T(8,128)S(1)}, f32[8,128]{1,0:T(8,128)S(1)}) custom-call(s32[2]{0:T(128)S(1)} %pad_add_fusion.1.owners_ref, f32[8,128]{1,0:T(8,128)S(1)} %get-tuple-element.50.facts_ref.before_ref, bf16[1024,1536]{1,0:T(8,128)(2,1)S(1)} %get-tuple-element.101.x0_ref, bf16[1024,512]{1,0:T(8,128)(2,1)} %bitcast.10.x1_ref), custom_call_target="tpu_custom_call" | custom-call | tf_op jit(solution)/shard_map/pallas_call | solution.py:99
  150.9 1.3 collective-permute-start.6
  152.3 2.1 %collective-permute-start.7 = (f16[464,512]{1,0:T(8,128)(2,1)S(1)}, f16[464,512]{1,0:T(8,128)(2,1)S(1)}, u32[]{:S(2)}, u32[]{:S(2)}) collective-permute-start(f16[464,512]{1,0:T(8,128)(2,1)S(1)} %convert_element_type.181), channel_id=1, source_target_pairs={{0,3},{1,0},{2,1},{3,2},{4,7},{5,4},{6,5},{7,6},{8,11},{9,8},{10,9... | collective-permute-start | bytes 1425416 | tf_op jit(solution)/shard_map/ppermute | solution.py:244
  154.4 2.6 %shard_map.35 = (f32[464,512]{1,0:T(8,128)S(1)}, f32[464,512]{1,0:T(8,128)S(1)}) custom-call(s32[2]{0:T(128)S(1)} %get-tuple-element.122.owners_ref, f32[8,128]{1,0:T(8,128)S(1)} %get-tuple-element.62.facts_ref, bf16[1024,1536]{1,0:T(8,128)(2,1)S(1)} %get-tuple-element.101.x0_ref, bf16[1024,512]{1,0:T(8,128)(2,1)} %bitcast.10.x1_ref), custom_call_target="tpu_custom_call" | custom-call | tf_op jit(solution)/shard_map/pallas_call | solution.py:99
  157.4 3.5 %collective-permute-start.9 = (f16[464,512]{1,0:T(8,128)(2,1)S(1)}, f16[464,512]{1,0:T(8,128)(2,1)S(1)}, u32[]{:S(2)}, u32[]{:S(2)}) collective-permute-start(f16[464,512]{1,0:T(8,128)(2,1)S(1)} %convert_element_type.183), channel_id=1, source_target_pairs={{0,3},{1,0},{2,1},{3,2},{4,7},{5,4},{6,5},{7,6},{8,11},{9,8},{10,9... | collective-permute-start | bytes 1425416 | tf_op jit(solution)/shard_map/ppermute | solution.py:244
  160.9 0.8 multiply_reduce_fusion.5
  161.8 1.0 multiply_reduce_fusion.3
  162.7 1.9 %add_multiply_fusion = (f32[192,1536]{1,0:T(8,128)S(1)}, f32[192,1536]{1,0:T(8,128)S(1)}) fusion(f32[208,1536]{1,0:T(8,128)S(1)} %copy-done.1, f32[1536]{0:T(1024)S(1)} %get-tuple-element.111, f16[208,1536]{1,0:T(8,128)(2,1)} %collective-permute-done.5, f32[1536]{0:T(1024)S(1)} %get-tuple-element.110, f16[208,1536]{1,0:T(8,128)(2,1)S(1)} %copy-done.5, ...), kind=kLoop, calls=%fused_computation.2 | loop fusion | flops 4718592 | bytes 7120896 | tf_op jit(solution)/shard_map/mul | solution.py:355
  164.7 1.5 shard_map.38.before_ref
  166.3 2.5 %shard_map.34 = (f32[464,512]{1,0:T(8,128)S(1)}, f32[464,512]{1,0:T(8,128)S(1)}) custom-call(s32[2]{0:T(128)S(1)} %pad_add_fusion.owners_ref, f32[8,128]{1,0:T(8,128)S(1)} %get-tuple-element.62.facts_ref, bf16[1024,1536]{1,0:T(8,128)(2,1)S(1)} %get-tuple-element.101.x0_ref, bf16[1024,512]{1,0:T(8,128)(2,1)} %bitcast.10.x1_ref), custom_call_target="tpu_custom_call" | custom-call | tf_op jit(solution)/shard_map/pallas_call | solution.py:99
  168.8 2.6 %shard_map.36 = (f32[464,512]{1,0:T(8,128)S(1)}, f32[464,512]{1,0:T(8,128)S(1)}) custom-call(s32[2]{0:T(128)S(1)} %get-tuple-element.123.owners_ref, f32[8,128]{1,0:T(8,128)S(1)} %get-tuple-element.62.facts_ref, bf16[1024,1536]{1,0:T(8,128)(2,1)S(1)} %get-tuple-element.101.x0_ref, bf16[1024,512]{1,0:T(8,128)(2,1)} %bitcast.10.x1_ref), custom_call_target="tpu_custom_call" | custom-call | tf_op jit(solution)/shard_map/pallas_call | solution.py:99
  171.5 0.7 select_convert_fusion.2
  172.2 2.2 %collective-permute-done.8 = f16[464,512]{1,0:T(8,128)(2,1)S(1)} collective-permute-done((f16[464,512]{1,0:T(8,128)(2,1)S(1)}, f16[464,512]{1,0:T(8,128)(2,1)S(1)}, u32[]{:S(2)}, u32[]{:S(2)}) %collective-permute-start.8) | collective-permute-done | bytes 475168 | tf_op jit(solution)/shard_map/ppermute | solution.py:244
  174.4 3.1 %collective-permute-start.11 = (f16[464,512]{1,0:T(8,128)(2,1)S(1)}, f16[464,512]{1,0:T(8,128)(2,1)S(1)}, u32[]{:S(2)}, u32[]{:S(2)}) collective-permute-start(f16[464,512]{1,0:T(8,128)(2,1)S(1)} %get-tuple-element.79), channel_id=1, source_target_pairs={{0,3},{1,0},{2,1},{3,2},{4,7},{5,4},{6,5},{7,6},{8,11},{9,8},{10,9... | collective-permute-start | bytes 1425416 | tf_op jit(solution)/shard_map/ppermute | solution.py:244
  177.7 8.2 %collective-permute-done.11 = f16[464,512]{1,0:T(8,128)(2,1)S(1)} collective-permute-done((f16[464,512]{1,0:T(8,128)(2,1)S(1)}, f16[464,512]{1,0:T(8,128)(2,1)S(1)}, u32[]{:S(2)}, u32[]{:S(2)}) %collective-permute-start.11) | collective-permute-done | bytes 475168 | tf_op jit(solution)/shard_map/ppermute | solution.py:244
  185.8 3.5 %collective-permute-done.10 = f16[464,512]{1,0:T(8,128)(2,1)S(1)} collective-permute-done((f16[464,512]{1,0:T(8,128)(2,1)S(1)}, f16[464,512]{1,0:T(8,128)(2,1)S(1)}, u32[]{:S(2)}, u32[]{:S(2)}) %collective-permute-start.10) | collective-permute-done | bytes 475168 | tf_op jit(solution)/shard_map/ppermute | solution.py:244
  189.9 1.4 shard_map.39
  (50 shorter events, 2.1 us)
Async XLA Ops:
  7.8 84.5 %all-to-all-start = ((bf16[64,16,1536]{2,1,0:T(8,128)(2,1)}), bf16[64,16,1536]{2,1,0:T(8,128)(2,1)S(1)}, u32[]{:S(2)}, u32[]{:S(2)}) async-start(bf16[64,16,1536]{2,1,0:T(8,128)(2,1)} %bitcast.36), calls=%async_computation | async-start | bytes 6291456 | tf_op jit(solution)/shard_map/all_to_all | solution.py:304
  96.1 18.7 %collective-permute-start.2 = (f16[208,1536]{1,0:T(8,128)(2,1)}, f16[208,1536]{1,0:T(8,128)(2,1)}, u32[]{:S(2)}, u32[]{:S(2)}) collective-permute-start(f16[208,1536]{1,0:T(8,128)(2,1)} %convert_element_type.168), channel_id=1, source_target_pairs={{0,1},{1,2},{2,3},{3,0},{4,5},{5,6},{6,7},{7,4},{8,9},{9,10},{10,1... | collective-permute-start | bytes 1916936 | tf_op jit(solution)/shard_map/ppermute | solution.py:244
  98.5 17.6 %collective-permute-start.3 = (f16[208,1536]{1,0:T(8,128)(2,1)}, f16[208,1536]{1,0:T(8,128)(2,1)}, u32[]{:S(2)}, u32[]{:S(2)}) collective-permute-start(f16[208,1536]{1,0:T(8,128)(2,1)} %convert_element_type.169), channel_id=1, source_target_pairs={{0,3},{1,0},{2,1},{3,2},{4,7},{5,4},{6,5},{7,6},{8,11},{9,8},{10,9... | collective-permute-start | bytes 1916936 | tf_op jit(solution)/shard_map/ppermute | solution.py:244
  100.2 48.0 %all-to-all-start.1 = ((bf16[64,16,512]{2,1,0:T(8,128)(2,1)}), bf16[64,16,512]{2,1,0:T(8,128)(2,1)}, u32[]{:S(2)}, u32[]{:S(2)}) async-start(bf16[64,16,512]{2,1,0:T(8,128)(2,1)} %bitcast.37), calls=%async_computation.1 | async-start | bytes 2097152 | tf_op jit(solution)/shard_map/all_to_all | solution.py:304
  109.8 18.6 %collective-permute-start = (f16[208,1536]{1,0:T(8,128)(2,1)S(1)}, f16[208,1536]{1,0:T(8,128)(2,1)S(1)}, u32[]{:S(2)}, u32[]{:S(2)}) collective-permute-start(f16[208,1536]{1,0:T(8,128)(2,1)S(1)} %convert_element_type.166), channel_id=1, source_target_pairs={{0,1},{1,2},{2,3},{3,0},{4,5},{5,6},{6,7},{7,4},{8,9},{9,10},{10,1... | collective-permute-start | bytes 1916936 | tf_op jit(solution)/shard_map/ppermute | solution.py:244
  110.4 19.1 %collective-permute-start.1 = (f16[208,1536]{1,0:T(8,128)(2,1)S(1)}, f16[208,1536]{1,0:T(8,128)(2,1)S(1)}, u32[]{:S(2)}, u32[]{:S(2)}) collective-permute-start(f16[208,1536]{1,0:T(8,128)(2,1)S(1)} %convert_element_type.167), channel_id=1, source_target_pairs={{0,3},{1,0},{2,1},{3,2},{4,7},{5,4},{6,5},{7,6},{8,11},{9,8},{10,9... | collective-permute-start | bytes 1916936 | tf_op jit(solution)/shard_map/ppermute | solution.py:244
  128.5 1.0 copy-start.4
  129.5 0.8 copy-start.6
  130.3 17.9 %collective-permute-start.4 = (f16[208,1536]{1,0:T(8,128)(2,1)}, f16[208,1536]{1,0:T(8,128)(2,1)}, u32[]{:S(2)}, u32[]{:S(2)}) collective-permute-start(f16[208,1536]{1,0:T(8,128)(2,1)} %get-tuple-element.55), channel_id=1, source_target_pairs={{0,1},{1,2},{2,3},{3,0},{4,5},{5,6},{6,7},{7,4},{8,9},{9,10},{10,1... | collective-permute-start | bytes 1916936 | tf_op jit(solution)/shard_map/ppermute | solution.py:244
  131.8 16.4 %collective-permute-start.5 = (f16[208,1536]{1,0:T(8,128)(2,1)}, f16[208,1536]{1,0:T(8,128)(2,1)}, u32[]{:S(2)}, u32[]{:S(2)}) collective-permute-start(f16[208,1536]{1,0:T(8,128)(2,1)} %get-tuple-element.56), channel_id=1, source_target_pairs={{0,3},{1,0},{2,1},{3,2},{4,7},{5,4},{6,5},{7,6},{8,11},{9,8},{10,9... | collective-permute-start | bytes 1916936 | tf_op jit(solution)/shard_map/ppermute | solution.py:244
  135.6 1.0 copy-start
  136.7 1.0 copy-start.2
  150.9 15.3 %collective-permute-start.6 = (f16[464,512]{1,0:T(8,128)(2,1)S(1)}, f16[464,512]{1,0:T(8,128)(2,1)S(1)}, u32[]{:S(2)}, u32[]{:S(2)}) collective-permute-start(f16[464,512]{1,0:T(8,128)(2,1)S(1)} %convert_element_type.180), channel_id=1, source_target_pairs={{0,1},{1,2},{2,3},{3,0},{4,5},{5,6},{6,7},{7,4},{8,9},{9,10},{10,1... | collective-permute-start | bytes 1425416 | tf_op jit(solution)/shard_map/ppermute | solution.py:244
  152.3 14.0 %collective-permute-start.7 = (f16[464,512]{1,0:T(8,128)(2,1)S(1)}, f16[464,512]{1,0:T(8,128)(2,1)S(1)}, u32[]{:S(2)}, u32[]{:S(2)}) collective-permute-start(f16[464,512]{1,0:T(8,128)(2,1)S(1)} %convert_element_type.181), channel_id=1, source_target_pairs={{0,3},{1,0},{2,1},{3,2},{4,7},{5,4},{6,5},{7,6},{8,11},{9,8},{10,9... | collective-permute-start | bytes 1425416 | tf_op jit(solution)/shard_map/ppermute | solution.py:244
  154.4 7.3 %copy-start.5 = (f16[208,1536]{1,0:T(8,128)(2,1)S(1)}, f16[208,1536]{1,0:T(8,128)(2,1)}, u32[]{:S(2)}) copy-start(f16[208,1536]{1,0:T(8,128)(2,1)} %copy-done.4) | copy-start | bytes 1916932
  154.4 8.3 %copy-start.7 = (f16[208,1536]{1,0:T(8,128)(2,1)S(1)}, f16[208,1536]{1,0:T(8,128)(2,1)}, u32[]{:S(2)}) copy-start(f16[208,1536]{1,0:T(8,128)(2,1)} %copy-done.6) | copy-start | bytes 1916932
  157.1 4.7 %copy-start.1 = (f32[208,1536]{1,0:T(8,128)S(1)}, f32[208,1536]{1,0:T(8,128)}, u32[]{:S(2)}) copy-start(f32[208,1536]{1,0:T(8,128)} %copy-done) | copy-start | bytes 3833860
  157.1 5.6 %copy-start.3 = (f32[208,1536]{1,0:T(8,128)S(1)}, f32[208,1536]{1,0:T(8,128)}, u32[]{:S(2)}) copy-start(f32[208,1536]{1,0:T(8,128)} %copy-done.2) | copy-start | bytes 3833860
  157.2 17.2 %collective-permute-start.8 = (f16[464,512]{1,0:T(8,128)(2,1)S(1)}, f16[464,512]{1,0:T(8,128)(2,1)S(1)}, u32[]{:S(2)}, u32[]{:S(2)}) collective-permute-start(f16[464,512]{1,0:T(8,128)(2,1)S(1)} %convert_element_type.182), channel_id=1, source_target_pairs={{0,1},{1,2},{2,3},{3,0},{4,5},{5,6},{6,7},{7,4},{8,9},{9,10},{10,1... | collective-permute-start | bytes 1425416 | tf_op jit(solution)/shard_map/ppermute | solution.py:244
  157.4 17.0 %collective-permute-start.9 = (f16[464,512]{1,0:T(8,128)(2,1)S(1)}, f16[464,512]{1,0:T(8,128)(2,1)S(1)}, u32[]{:S(2)}, u32[]{:S(2)}) collective-permute-start(f16[464,512]{1,0:T(8,128)(2,1)S(1)} %convert_element_type.183), channel_id=1, source_target_pairs={{0,3},{1,0},{2,1},{3,2},{4,7},{5,4},{6,5},{7,6},{8,11},{9,8},{10,9... | collective-permute-start | bytes 1425416 | tf_op jit(solution)/shard_map/ppermute | solution.py:244
  174.4 11.4 %collective-permute-start.11 = (f16[464,512]{1,0:T(8,128)(2,1)S(1)}, f16[464,512]{1,0:T(8,128)(2,1)S(1)}, u32[]{:S(2)}, u32[]{:S(2)}) collective-permute-start(f16[464,512]{1,0:T(8,128)(2,1)S(1)} %get-tuple-element.79), channel_id=1, source_target_pairs={{0,3},{1,0},{2,1},{3,2},{4,7},{5,4},{6,5},{7,6},{8,11},{9,8},{10,9... | collective-permute-start | bytes 1425416 | tf_op jit(solution)/shard_map/ppermute | solution.py:244
  177.5 11.8 %collective-permute-start.10 = (f16[464,512]{1,0:T(8,128)(2,1)S(1)}, f16[464,512]{1,0:T(8,128)(2,1)S(1)}, u32[]{:S(2)}, u32[]{:S(2)}) collective-permute-start(f16[464,512]{1,0:T(8,128)(2,1)S(1)} %get-tuple-element.70), channel_id=1, source_target_pairs={{0,1},{1,2},{2,3},{3,0},{4,5},{5,6},{6,7},{7,4},{8,9},{9,10},{10,1... | collective-permute-start | bytes 1425416 | tf_op jit(solution)/shard_map/ppermute | solution.py:244

commit v3 on v2

--- a/solution.py
+++ b/solution.py
@@ -106,7 +106,9 @@
     )(owners, *arrays)
 
 
-def pack_kernel(marked, start, slots_ref, activations_ref, out_ref, rows_ref, placed_ref, in_sem, out_sem):
+def pack_kernel(
+    marked, start, across_ref, down_ref, activations_ref, out_ref, rows_ref, placed_ref, in_sem, out_sem
+):
     strip = activations_ref.shape[1] // 4
     wide = out_ref.shape[1] // 4
     fetches = [
@@ -119,8 +121,21 @@
     ]
     for fetch in fetches:
         fetch.start()
-    shape = (out_ref.shape[0], slots_ref.shape[1])
-    chosen = slots_ref[...] == lax.broadcasted_iota(jnp.int32, shape, 0)
+    blocks, rows = across_ref.shape[1], activations_ref.shape[0]
+    block_rows = rows // blocks
+    earlier = lax.broadcasted_iota(jnp.int32, (blocks, blocks), 0) < lax.broadcasted_iota(
+        jnp.int32, (blocks, blocks), 1
+    )
+    again = jnp.where(earlier & (down_ref[...] == across_ref[...]), 1, 0)
+    slots = across_ref[...] * 2 + jnp.sum(again, axis=0, keepdims=True)
+    row = lax.broadcasted_iota(jnp.int32, (blocks, rows), 1)
+    spread = row // block_rows == lax.broadcasted_iota(jnp.int32, (blocks, rows), 0)
+    slots = jnp.broadcast_to(slots.astype(jnp.float32), (8, blocks)).astype(jnp.bfloat16)
+    spread = jnp.where(spread, 1.0, 0.0).astype(jnp.bfloat16)
+    slots = jnp.dot(slots, spread, preferred_element_type=jnp.float32)[:1].astype(jnp.int32)
+    slots = slots * block_rows + row[:1] % block_rows
+    shape = (out_ref.shape[0], rows)
+    chosen = slots == lax.broadcasted_iota(jnp.int32, shape, 0)
     selector = jnp.where(chosen, 1.0, 0.0).astype(jnp.bfloat16)
     stores = []
     for d in range(4):
@@ -140,12 +155,12 @@
         store.wait()
 
 
-def pack(activations, slots, rows, start, wide, marked):
-    hbm = pl.BlockSpec(memory_space=pltpu.HBM)
+def pack(activations, targets, rows, start, wide, marked):
+    hbm, vmem = pl.BlockSpec(memory_space=pltpu.HBM), pl.BlockSpec(memory_space=pltpu.VMEM)
     return pl.pallas_call(
         functools.partial(pack_kernel, marked, start),
         out_shape=jax.ShapeDtypeStruct((rows, 4 * wide), jnp.bfloat16),
-        in_specs=[pl.BlockSpec(memory_space=pltpu.VMEM), hbm],
+        in_specs=[vmem, vmem, hbm],
         out_specs=hbm,
         scratch_shapes=[
             pltpu.VMEM((4, activations.shape[0], wide), jnp.bfloat16),
@@ -154,7 +169,7 @@
             pltpu.SemaphoreType.DMA((4,)),
         ],
         compiler_params=pltpu.CompilerParams(vmem_limit_bytes=60 * 1024 * 1024),
-    )(slots, activations)
+    )(targets.reshape(1, -1), targets.reshape(-1, 1), activations)
 
 
 def copies(pieces, sem):
@@ -230,12 +245,12 @@
         upper, lower, facts = far()
         self.far = self.send(upper, 1), self.send(lower, -1)
         behind, ahead = grams(facts, -1, 1)
-        self.direct = self.send(ahead, 1), self.send(behind, -1)
+        near = ahead.astype(WIRE), behind.astype(WIRE)
+        self.direct = self.send(near[0], 1), self.send(near[1], -1)
         self.facts = facts
-        far, facts = lax.optimization_barrier((self.far, facts))
+        far, facts, _ = lax.optimization_barrier((self.far, facts, near))
         ahead, behind = grams(facts, 1, -1)
         merged = self.merge(ahead, far[0]).astype(WIRE), self.merge(behind, far[1]).astype(WIRE)
-        self.direct, merged = lax.optimization_barrier((self.direct, merged))
         self.merged = self.send(merged[0], 1), self.send(merged[1], -1)
         self.own = grams(facts, 0, 0)
 
@@ -275,8 +290,7 @@
 
 
 def on_device(activations, destination):
-    targets = destination[:, 0]
-    block_count = targets.shape[0]
+    block_count = destination.shape[0]
     rows, width = activations.shape
     block_rows = rows // block_count
     groups = lax.axis_size("expert")
@@ -287,17 +301,8 @@
     slot_rows = groups * capacity * block_rows
     me = lax.axis_index("blk")
 
-    positions = jnp.arange(block_count, dtype=jnp.int32)
-    same_target = targets[:, None] == targets[None, :]
-    earlier = positions[None, :] < positions[:, None]
-    ranking = jnp.sum((same_target & earlier).astype(jnp.int32), axis=1)
-    slots = targets * capacity + ranking
-    row_slots = (
-        slots[:, None] * block_rows + jnp.arange(block_rows, dtype=jnp.int32)[None, :]
-    ).reshape(1, rows)
-
     def packed(start, stop, marked):
-        placed = pack(activations, row_slots, slot_rows, start, stop - start, marked)
+        placed = pack(activations, destination, slot_rows, start, stop - start, marked)
         return placed.reshape(groups, capacity * block_rows, placed.shape[1])
 
     def routed(x):
@@ -337,7 +342,9 @@
         ),
         ranks,
     )
-    ring0.merged, x1 = lax.optimization_barrier((ring0.merged, x1))
+    (ring0.direct, ring0.merged), x1 = lax.optimization_barrier(
+        ((ring0.direct, ring0.merged), x1)
+    )
     ring1 = Ring(
         lambda: partial_grams(
             second_far, half1, ranks * last, owners((2, 2)), ring0.facts, x0, x1, facts=True

time: 193 us -> 184 us (0.953)
  waiting for transfers between devices: 100 us -> 91.7 us
    ppermute x12, waiting for transfers between devices: 33 us -> 24.7 us  [send(): return lax.ppermute(values.astype(WIRE), 'blk', pairs)]
    convert_element_type x0 -> x4, other arithmetic: none -> 2.02 us  [__init__(): near = (ahead.astype(WIRE), behind.astype(WIRE))]
  transfers between devices with their start and end apart: 14 -> 14, of which waited for: 9 -> 7; matrix products, arithmetic and copies ran while one was open for 6% -> 8% of each run, Pallas kernels for 11% -> 11%
where the time goes in v3:
time: 184 us; the launch traced here: 183 us
  waiting for transfers between devices  91.7 us (50%)
  starting transfers between devices  38.3 us (21%)
  Pallas kernels  32.7 us (18%)
  other arithmetic  16.2 us (9%)
  local copies, waits for them, and re-layouts  3.44 us (2%)
    all_to_all x2, waiting for transfers between devices, routed(): got = lax.all_to_all(x, 'expert', split_axis=0, concat_axis=0, tiled=True)  67 us
    ppermute x12, waiting for transfers between devices, send(): return lax.ppermute(values.astype(WIRE), 'blk', pairs)  24.7 us
    all_to_all x2, starting transfers between devices, routed(): got = lax.all_to_all(x, 'expert', split_axis=0, concat_axis=0, tiled=True)  19.5 us
    pallas_call x8, Pallas kernels, partial_grams(): pl.pallas_call(kernel, out_shape=shapes, in_specs=[smem] + [vmem] * len(a...  18.9 us
    ppermute x12, starting transfers between devices, send(): return lax.ppermute(values.astype(WIRE), 'blk', pairs)  18.8 us
    pallas_call x2, Pallas kernels, pack(): pl.pallas_call(functools.partial(pack_kernel, marked, start), out_shape=j...  10.9 us
    convert_element_type x2, other arithmetic, __init__(): self.merge(behind, far[1]).astype(WIRE)  4.06 us
  transfers between devices with their start and end apart: 14, of which 7 were waited for; matrix products, arithmetic and copies ran while one was open for 8% of the time, Pallas kernels for 11%

profile of v3, /device:TPU:8, one launch (start us, length us, event | category | flops | bytes accessed | tf_op | source)
XLA Modules:
  0.0 182.8 jit_solution(6445006517896663258)
XLA Ops:
  0.0 1.3 copy.4.down_ref
  1.3 5.6 %shard_map.28 = bf16[1024,1536]{1,0:T(8,128)(2,1)} custom-call(s32[1,64]{1,0:T(1,128)} %bitcast.47, s32[64,1]{1,0:T(8,128)} %copy.4.down_ref, bf16[512,2048]{1,0:T(8,128)(2,1)} %activations_ref.3), custom_call_target="tpu_custom_call" | custom-call | tf_op jit(solution)/shard_map/pallas_call | solution.py:160
  6.9 12.1 %all-to-all-start = ((bf16[64,16,1536]{2,1,0:T(8,128)(2,1)}), bf16[64,16,1536]{2,1,0:T(8,128)(2,1)S(1)}, u32[]{:S(2)}, u32[]{:S(2)}) async-start(bf16[64,16,1536]{2,1,0:T(8,128)(2,1)} %bitcast.28), calls=%async_computation | async-start | bytes 6291456 | tf_op jit(solution)/shard_map/all_to_all | solution.py:309
  19.1 5.3 %shard_map.29 = bf16[1024,512]{1,0:T(8,128)(2,1)} custom-call(s32[1,64]{1,0:T(1,128)} %bitcast.48, s32[64,1]{1,0:T(8,128)} %copy.4.down_ref, bf16[512,2048]{1,0:T(8,128)(2,1)} %activations_ref.3), custom_call_target="tpu_custom_call" | custom-call | tf_op jit(solution)/shard_map/pallas_call | solution.py:160
  24.4 67.0 %all-to-all-done = bf16[64,16,1536]{2,1,0:T(8,128)(2,1)S(1)} async-done(((bf16[64,16,1536]{2,1,0:T(8,128)(2,1)}), bf16[64,16,1536]{2,1,0:T(8,128)(2,1)S(1)}, u32[]{:S(2)}, u32[]{:S(2)}) %all-to-all-start) | async-done | bytes 3145760 | tf_op jit(solution)/shard_map/all_to_all | solution.py:309
  91.6 2.6 %shard_map.30 = (f32[208,1536]{1,0:T(8,128)S(1)}, f32[208,1536]{1,0:T(8,128)S(1)}, f32[8,128]{1,0:T(8,128)S(1)}) custom-call(s32[2]{0:T(128)S(1)} %pad_add_fusion.1.owners_ref, bf16[1024,128]{1,0:T(8,128)(2,1)S(1)} %get-tuple-element.90.corner_ref, bf16[1024,1536]{1,0:T(8,128)(2,1)S(1)} %get-tuple-element.89.x0_ref), custom_call_target="tpu_custom_call" | custom-call | tf_op jit(solution)/shard_map/pallas_call | solution.py:99
  94.3 0.9 convert_element_type.164
  95.2 1.5 collective-permute-start.2
  96.7 0.9 convert_element_type.165
  97.6 1.8 collective-permute-start.3
  99.3 7.4 %all-to-all-start.1 = ((bf16[64,16,512]{2,1,0:T(8,128)(2,1)}), bf16[64,16,512]{2,1,0:T(8,128)(2,1)}, u32[]{:S(2)}, u32[]{:S(2)}) async-start(bf16[64,16,512]{2,1,0:T(8,128)(2,1)} %bitcast.29), calls=%async_computation.1 | async-start | bytes 2097152 | tf_op jit(solution)/shard_map/all_to_all | solution.py:309
  106.8 2.0 %shard_map.31 = (f32[208,1536]{1,0:T(8,128)S(1)}, f32[208,1536]{1,0:T(8,128)S(1)}) custom-call(s32[2]{0:T(128)S(1)} %get-tuple-element.110.owners_ref, f32[8,128]{1,0:T(8,128)S(1)} %get-tuple-element.44.facts_ref.before_ref, bf16[1024,1536]{1,0:T(8,128)(2,1)S(1)} %get-tuple-element.89.x0_ref), custom_call_target="tpu_custom_call" | custom-call | tf_op jit(solution)/shard_map/pallas_call | solution.py:99
  108.8 0.9 convert_element_type.162
  109.8 0.3 collective-permute-start
  110.0 0.9 convert_element_type.163
  111.0 3.0 %collective-permute-start.1 = (f16[208,1536]{1,0:T(8,128)(2,1)}, f16[208,1536]{1,0:T(8,128)(2,1)}, u32[]{:S(2)}, u32[]{:S(2)}) collective-permute-start(f16[208,1536]{1,0:T(8,128)(2,1)} %convert_element_type.163), channel_id=1, source_target_pairs={{0,3},{1,0},{2,1},{3,2},{4,7},{5,4},{6,5},{7,6},{8,11},{9,8},{10,9... | collective-permute-start | bytes 1916936 | tf_op jit(solution)/shard_map/ppermute | solution.py:259
  113.9 1.2 collective-permute-done.3
  115.2 2.0 %shard_map.32 = (f32[208,1536]{1,0:T(8,128)S(1)}, f32[208,1536]{1,0:T(8,128)S(1)}) custom-call(s32[2]{0:T(128)S(1)} %get-tuple-element.111.owners_ref, f32[8,128]{1,0:T(8,128)S(1)} %get-tuple-element.44.facts_ref.before_ref, bf16[1024,1536]{1,0:T(8,128)(2,1)S(1)} %get-tuple-element.89.x0_ref), custom_call_target="tpu_custom_call" | custom-call | tf_op jit(solution)/shard_map/pallas_call | solution.py:99
  117.2 1.0 select_reduce_fusion.1
  118.1 1.0 select_reduce_fusion.3
  119.1 3.4 %select_convert_fusion = (f16[208,1536]{1,0:T(8,128)(2,1)}, f16[208,1536]{1,0:T(8,128)(2,1)}) fusion(f16[208,1536]{1,0:T(8,128)(2,1)} %collective-permute-done.3, f32[208,1536]{1,0:T(8,128)S(1)} %get-tuple-element.47, f32[1536]{0:T(1024)S(1)} %get-tuple-element.75, f32[1536]{0:T(1024)S(1)} %get-tuple-element.72, f32[1536]{0:T(1024)S(1)} %get-tuple-element.71, ...), kind=kLoop, calls=%fused_computation | loop fusion | flops 5111808 | bytes 5173872 | tf_op jit(solution)/shard_map/convert_element_type | solution.py:253
  122.5 1.5 collective-permute-start.4
  124.0 1.8 collective-permute-start.5
  125.8 2.0 %shard_map.37 = (f32[208,1536]{1,0:T(8,128)S(1)}, f32[208,1536]{1,0:T(8,128)S(1)}) custom-call(s32[2]{0:T(128)S(1)} %pad_add_fusion.owners_ref, f32[8,128]{1,0:T(8,128)S(1)} %get-tuple-element.44.facts_ref.before_ref, bf16[1024,1536]{1,0:T(8,128)(2,1)S(1)} %get-tuple-element.89.x0_ref), custom_call_target="tpu_custom_call" | custom-call | tf_op jit(solution)/shard_map/pallas_call | solution.py:99
  127.8 1.0 copy-done
  128.9 1.0 copy-done.2
  129.9 11.5 %collective-permute-done.4 = f16[208,1536]{1,0:T(8,128)(2,1)} collective-permute-done((f16[208,1536]{1,0:T(8,128)(2,1)}, f16[208,1536]{1,0:T(8,128)(2,1)}, u32[]{:S(2)}, u32[]{:S(2)}) %collective-permute-start.4) | collective-permute-done | bytes 639008 | tf_op jit(solution)/shard_map/ppermute | solution.py:259
  141.4 1.0 collective-permute-done.5
  142.4 2.6 %shard_map.33 = (f32[464,512]{1,0:T(8,128)S(1)}, f32[464,512]{1,0:T(8,128)S(1)}, f32[8,128]{1,0:T(8,128)S(1)}) custom-call(s32[2]{0:T(128)S(1)} %pad_add_fusion.1.owners_ref, f32[8,128]{1,0:T(8,128)S(1)} %get-tuple-element.44.facts_ref.before_ref, bf16[1024,1536]{1,0:T(8,128)(2,1)S(1)} %get-tuple-element.89.x0_ref, bf16[1024,512]{1,0:T(8,128)(2,1)} %bitcast.8.x1_ref), custom_call_target="tpu_custom_call" | custom-call | tf_op jit(solution)/shard_map/pallas_call | solution.py:99
  145.1 1.5 collective-permute-start.6
  146.8 1.9 %collective-permute-start.7 = (f16[464,512]{1,0:T(8,128)(2,1)S(1)}, f16[464,512]{1,0:T(8,128)(2,1)S(1)}, u32[]{:S(2)}, u32[]{:S(2)}) collective-permute-start(f16[464,512]{1,0:T(8,128)(2,1)S(1)} %convert_element_type.177), channel_id=1, source_target_pairs={{0,3},{1,0},{2,1},{3,2},{4,7},{5,4},{6,5},{7,6},{8,11},{9,8},{10,9... | collective-permute-start | bytes 1425416 | tf_op jit(solution)/shard_map/ppermute | solution.py:259
  148.6 2.6 %shard_map.34 = (f32[464,512]{1,0:T(8,128)S(1)}, f32[464,512]{1,0:T(8,128)S(1)}) custom-call(s32[2]{0:T(128)S(1)} %get-tuple-element.110.owners_ref, f32[8,128]{1,0:T(8,128)S(1)} %get-tuple-element.56.facts_ref, bf16[1024,1536]{1,0:T(8,128)(2,1)S(1)} %get-tuple-element.89.x0_ref, bf16[1024,512]{1,0:T(8,128)(2,1)} %bitcast.8.x1_ref), custom_call_target="tpu_custom_call" | custom-call | tf_op jit(solution)/shard_map/pallas_call | solution.py:99
  151.4 0.3 collective-permute-start.10
  151.7 3.0 %collective-permute-start.9 = (f16[464,512]{1,0:T(8,128)(2,1)S(1)}, f16[464,512]{1,0:T(8,128)(2,1)S(1)}, u32[]{:S(2)}, u32[]{:S(2)}) collective-permute-start(f16[464,512]{1,0:T(8,128)(2,1)S(1)} %convert_element_type.179), channel_id=1, source_target_pairs={{0,3},{1,0},{2,1},{3,2},{4,7},{5,4},{6,5},{7,6},{8,11},{9,8},{10,9... | collective-permute-start | bytes 1425416 | tf_op jit(solution)/shard_map/ppermute | solution.py:259
  154.7 0.8 multiply_reduce_fusion.4
  155.5 0.8 multiply_reduce_fusion.5
  156.4 1.0 multiply_reduce_fusion.3
  157.4 2.3 %add_multiply_fusion = (f32[192,1536]{1,0:T(8,128)S(1)}, f32[192,1536]{1,0:T(8,128)S(1)}) fusion(f32[208,1536]{1,0:T(8,128)S(1)} %copy-done.1, f32[1536]{0:T(1024)S(1)} %get-tuple-element.99, f16[208,1536]{1,0:T(8,128)(2,1)} %collective-permute-done.5, f32[1536]{0:T(1024)S(1)} %get-tuple-element.98, f16[208,1536]{1,0:T(8,128)(2,1)} %collective-permute-done, ...), kind=kLoop, calls=%fused_computation.2 | loop fusion | flops 4718592 | bytes 7120896 | tf_op jit(solution)/shard_map/mul | solution.py:362
  159.7 1.5 shard_map.38.before_ref
  161.3 2.5 %shard_map.36 = (f32[464,512]{1,0:T(8,128)S(1)}, f32[464,512]{1,0:T(8,128)S(1)}) custom-call(s32[2]{0:T(128)S(1)} %get-tuple-element.111.owners_ref, f32[8,128]{1,0:T(8,128)S(1)} %get-tuple-element.56.facts_ref, bf16[1024,1536]{1,0:T(8,128)(2,1)S(1)} %get-tuple-element.89.x0_ref, bf16[1024,512]{1,0:T(8,128)(2,1)} %bitcast.8.x1_ref), custom_call_target="tpu_custom_call" | custom-call | tf_op jit(solution)/shard_map/pallas_call | solution.py:99
  163.9 0.7 select_convert_fusion.2
  164.6 2.5 %shard_map.35 = (f32[464,512]{1,0:T(8,128)S(1)}, f32[464,512]{1,0:T(8,128)S(1)}) custom-call(s32[2]{0:T(128)S(1)} %pad_add_fusion.owners_ref, f32[8,128]{1,0:T(8,128)S(1)} %get-tuple-element.56.facts_ref, bf16[1024,1536]{1,0:T(8,128)(2,1)S(1)} %get-tuple-element.89.x0_ref, bf16[1024,512]{1,0:T(8,128)(2,1)} %bitcast.8.x1_ref), custom_call_target="tpu_custom_call" | custom-call | tf_op jit(solution)/shard_map/pallas_call | solution.py:99
  167.2 2.4 %collective-permute-start.11 = (f16[464,512]{1,0:T(8,128)(2,1)S(1)}, f16[464,512]{1,0:T(8,128)(2,1)S(1)}, u32[]{:S(2)}, u32[]{:S(2)}) collective-permute-start(f16[464,512]{1,0:T(8,128)(2,1)S(1)} %get-tuple-element.106), channel_id=1, source_target_pairs={{0,3},{1,0},{2,1},{3,2},{4,7},{5,4},{6,5},{7,6},{8,11},{9,8},{10,9... | collective-permute-start | bytes 1425416 | tf_op jit(solution)/shard_map/ppermute | solution.py:259
  169.6 0.6 collective-permute-done.9
  170.2 9.4 %collective-permute-done.11 = f16[464,512]{1,0:T(8,128)(2,1)S(1)} collective-permute-done((f16[464,512]{1,0:T(8,128)(2,1)S(1)}, f16[464,512]{1,0:T(8,128)(2,1)S(1)}, u32[]{:S(2)}, u32[]{:S(2)}) %collective-permute-start.11) | collective-permute-done | bytes 475168 | tf_op jit(solution)/shard_map/ppermute | solution.py:259
  179.7 1.1 collective-permute-done.8
  180.7 0.6 add_multiply_fusion.2
  181.3 1.4 shard_map.39
  (39 shorter events, 1.0 us)
Async XLA Ops:
  6.9 84.5 %all-to-all-start = ((bf16[64,16,1536]{2,1,0:T(8,128)(2,1)}), bf16[64,16,1536]{2,1,0:T(8,128)(2,1)S(1)}, u32[]{:S(2)}, u32[]{:S(2)}) async-start(bf16[64,16,1536]{2,1,0:T(8,128)(2,1)} %bitcast.28), calls=%async_computation | async-start | bytes 6291456 | tf_op jit(solution)/shard_map/all_to_all | solution.py:309
  95.2 18.7 %collective-permute-start.2 = (f16[208,1536]{1,0:T(8,128)(2,1)}, f16[208,1536]{1,0:T(8,128)(2,1)}, u32[]{:S(2)}, u32[]{:S(2)}) collective-permute-start(f16[208,1536]{1,0:T(8,128)(2,1)} %convert_element_type.164), channel_id=1, source_target_pairs={{0,1},{1,2},{2,3},{3,0},{4,5},{5,6},{6,7},{7,4},{8,9},{9,10},{10,1... | collective-permute-start | bytes 1916936 | tf_op jit(solution)/shard_map/ppermute | solution.py:259
  97.6 17.6 %collective-permute-start.3 = (f16[208,1536]{1,0:T(8,128)(2,1)}, f16[208,1536]{1,0:T(8,128)(2,1)}, u32[]{:S(2)}, u32[]{:S(2)}) collective-permute-start(f16[208,1536]{1,0:T(8,128)(2,1)} %convert_element_type.165), channel_id=1, source_target_pairs={{0,3},{1,0},{2,1},{3,2},{4,7},{5,4},{6,5},{7,6},{8,11},{9,8},{10,9... | collective-permute-start | bytes 1916936 | tf_op jit(solution)/shard_map/ppermute | solution.py:259
  99.3 43.0 %all-to-all-start.1 = ((bf16[64,16,512]{2,1,0:T(8,128)(2,1)}), bf16[64,16,512]{2,1,0:T(8,128)(2,1)}, u32[]{:S(2)}, u32[]{:S(2)}) async-start(bf16[64,16,512]{2,1,0:T(8,128)(2,1)} %bitcast.29), calls=%async_computation.1 | async-start | bytes 2097152 | tf_op jit(solution)/shard_map/all_to_all | solution.py:309
  109.8 20.2 %collective-permute-start = (f16[208,1536]{1,0:T(8,128)(2,1)}, f16[208,1536]{1,0:T(8,128)(2,1)}, u32[]{:S(2)}, u32[]{:S(2)}) collective-permute-start(f16[208,1536]{1,0:T(8,128)(2,1)} %convert_element_type.162), channel_id=1, source_target_pairs={{0,1},{1,2},{2,3},{3,0},{4,5},{5,6},{6,7},{7,4},{8,9},{9,10},{10,1... | collective-permute-start | bytes 1916936 | tf_op jit(solution)/shard_map/ppermute | solution.py:259
  111.0 19.0 %collective-permute-start.1 = (f16[208,1536]{1,0:T(8,128)(2,1)}, f16[208,1536]{1,0:T(8,128)(2,1)}, u32[]{:S(2)}, u32[]{:S(2)}) collective-permute-start(f16[208,1536]{1,0:T(8,128)(2,1)} %convert_element_type.163), channel_id=1, source_target_pairs={{0,3},{1,0},{2,1},{3,2},{4,7},{5,4},{6,5},{7,6},{8,11},{9,8},{10,9... | collective-permute-start | bytes 1916936 | tf_op jit(solution)/shard_map/ppermute | solution.py:259
  122.5 18.9 %collective-permute-start.4 = (f16[208,1536]{1,0:T(8,128)(2,1)}, f16[208,1536]{1,0:T(8,128)(2,1)}, u32[]{:S(2)}, u32[]{:S(2)}) collective-permute-start(f16[208,1536]{1,0:T(8,128)(2,1)} %get-tuple-element.109), channel_id=1, source_target_pairs={{0,1},{1,2},{2,3},{3,0},{4,5},{5,6},{6,7},{7,4},{8,9},{9,10},{10,1... | collective-permute-start | bytes 1916936 | tf_op jit(solution)/shard_map/ppermute | solution.py:259
  124.0 18.4 %collective-permute-start.5 = (f16[208,1536]{1,0:T(8,128)(2,1)}, f16[208,1536]{1,0:T(8,128)(2,1)}, u32[]{:S(2)}, u32[]{:S(2)}) collective-permute-start(f16[208,1536]{1,0:T(8,128)(2,1)} %get-tuple-element.108), channel_id=1, source_target_pairs={{0,3},{1,0},{2,1},{3,2},{4,7},{5,4},{6,5},{7,6},{8,11},{9,8},{10,9... | collective-permute-start | bytes 1916936 | tf_op jit(solution)/shard_map/ppermute | solution.py:259
  127.8 1.0 copy-start
  128.9 1.0 copy-start.2
  145.1 16.1 %collective-permute-start.6 = (f16[464,512]{1,0:T(8,128)(2,1)S(1)}, f16[464,512]{1,0:T(8,128)(2,1)S(1)}, u32[]{:S(2)}, u32[]{:S(2)}) collective-permute-start(f16[464,512]{1,0:T(8,128)(2,1)S(1)} %convert_element_type.176), channel_id=1, source_target_pairs={{0,1},{1,2},{2,3},{3,0},{4,5},{5,6},{6,7},{7,4},{8,9},{9,10},{10,1... | collective-permute-start | bytes 1425416 | tf_op jit(solution)/shard_map/ppermute | solution.py:259
  146.8 14.5 %collective-permute-start.7 = (f16[464,512]{1,0:T(8,128)(2,1)S(1)}, f16[464,512]{1,0:T(8,128)(2,1)S(1)}, u32[]{:S(2)}, u32[]{:S(2)}) collective-permute-start(f16[464,512]{1,0:T(8,128)(2,1)S(1)} %convert_element_type.177), channel_id=1, source_target_pairs={{0,3},{1,0},{2,1},{3,2},{4,7},{5,4},{6,5},{7,6},{8,11},{9,8},{10,9... | collective-permute-start | bytes 1425416 | tf_op jit(solution)/shard_map/ppermute | solution.py:259
  151.2 5.2 %copy-start.1 = (f32[208,1536]{1,0:T(8,128)S(1)}, f32[208,1536]{1,0:T(8,128)}, u32[]{:S(2)}) copy-start(f32[208,1536]{1,0:T(8,128)} %copy-done) | copy-start | bytes 3833860
  151.2 6.2 %copy-start.3 = (f32[208,1536]{1,0:T(8,128)S(1)}, f32[208,1536]{1,0:T(8,128)}, u32[]{:S(2)}) copy-start(f32[208,1536]{1,0:T(8,128)} %copy-done.2) | copy-start | bytes 3833860
  151.4 18.2 %collective-permute-start.10 = (f16[464,512]{1,0:T(8,128)(2,1)S(1)}, f16[464,512]{1,0:T(8,128)(2,1)S(1)}, u32[]{:S(2)}, u32[]{:S(2)}) collective-permute-start(f16[464,512]{1,0:T(8,128)(2,1)S(1)} %convert_element_type.178), channel_id=1, source_target_pairs={{0,1},{1,2},{2,3},{3,0},{4,5},{5,6},{6,7},{7,4},{8,9},{9,10},{10,1... | collective-permute-start | bytes 1425416 | tf_op jit(solution)/shard_map/ppermute | solution.py:259
  151.7 18.5 %collective-permute-start.9 = (f16[464,512]{1,0:T(8,128)(2,1)S(1)}, f16[464,512]{1,0:T(8,128)(2,1)S(1)}, u32[]{:S(2)}, u32[]{:S(2)}) collective-permute-start(f16[464,512]{1,0:T(8,128)(2,1)S(1)} %convert_element_type.179), channel_id=1, source_target_pairs={{0,3},{1,0},{2,1},{3,2},{4,7},{5,4},{6,5},{7,6},{8,11},{9,8},{10,9... | collective-permute-start | bytes 1425416 | tf_op jit(solution)/shard_map/ppermute | solution.py:259
  167.2 12.4 %collective-permute-start.11 = (f16[464,512]{1,0:T(8,128)(2,1)S(1)}, f16[464,512]{1,0:T(8,128)(2,1)S(1)}, u32[]{:S(2)}, u32[]{:S(2)}) collective-permute-start(f16[464,512]{1,0:T(8,128)(2,1)S(1)} %get-tuple-element.106), channel_id=1, source_target_pairs={{0,3},{1,0},{2,1},{3,2},{4,7},{5,4},{6,5},{7,6},{8,11},{9,8},{10,9... | collective-permute-start | bytes 1425416 | tf_op jit(solution)/shard_map/ppermute | solution.py:259
  169.6 11.1 %collective-permute-start.8 = (f16[464,512]{1,0:T(8,128)(2,1)S(1)}, f16[464,512]{1,0:T(8,128)(2,1)S(1)}, u32[]{:S(2)}, u32[]{:S(2)}) collective-permute-start(f16[464,512]{1,0:T(8,128)(2,1)S(1)} %get-tuple-element.107), channel_id=1, source_target_pairs={{0,1},{1,2},{2,3},{3,0},{4,5},{5,6},{6,7},{7,4},{8,9},{9,10},{10,1... | collective-permute-start | bytes 1425416 | tf_op jit(solution)/shard_map/ppermute | solution.py:259

commit v4 on v3

--- a/solution.py
+++ b/solution.py
@@ -250,8 +250,8 @@
         self.facts = facts
         far, facts, _ = lax.optimization_barrier((self.far, facts, near))
         ahead, behind = grams(facts, 1, -1)
-        merged = self.merge(ahead, far[0]).astype(WIRE), self.merge(behind, far[1]).astype(WIRE)
-        self.merged = self.send(merged[0], 1), self.send(merged[1], -1)
+        self.passed = self.merge(ahead, far[0]).astype(WIRE), self.merge(behind, far[1]).astype(WIRE)
+        self.merged = self.send(self.passed[0], 1), self.send(self.passed[1], -1)
         self.own = grams(facts, 0, 0)
 
     def send(self, values, step):
@@ -320,18 +320,6 @@
     is_mark = (corner > MARK / 2) & (lax.broadcasted_iota(jnp.int32, corner.shape, 1) == 0)
     x0 = lax.dynamic_update_slice(x0, jnp.where(is_mark, jnp.zeros_like(corner), corner), (0, 0))
 
-    def owners(offsets):
-        return jnp.stack([lax.rem(me + o + ranks, ranks) for o in offsets])
-
-    x0 = routed(packed(0, FIRST, True))
-    x0, later = lax.optimization_barrier((x0, packed(FIRST, strip, False)))
-    x1 = routed(later)
-
-    corner = x0[:, :128]
-    is_mark = (corner > MARK / 2) & (lax.broadcasted_iota(jnp.int32, corner.shape, 1) == 0)
-    empty_blocks = jnp.sum(is_mark.astype(jnp.float32)) / block_rows
-    x0 = lax.dynamic_update_slice(x0, jnp.where(is_mark, jnp.zeros_like(corner), corner), (0, 0))
-
     half0, half1 = FIRST // 2, FIRST + last // 2
     ring0 = Ring(
         lambda: partial_grams(
@@ -342,9 +330,7 @@
         ),
         ranks,
     )
-    (ring0.direct, ring0.merged), x1 = lax.optimization_barrier(
-        ((ring0.direct, ring0.merged), x1)
-    )
+    ring0.direct, _, x1 = lax.optimization_barrier((ring0.direct, ring0.passed, x1))
     ring1 = Ring(
         lambda: partial_grams(
             second_far, half1, ranks * last, owners((2, 2)), ring0.facts, x0, x1, facts=True

time: 184 us -> 178 us (0.967)
  waiting for transfers between devices: 91.7 us -> 85.4 us
    ppermute x12, waiting for transfers between devices: 24.7 us -> 14.5 us  [send(): return lax.ppermute(values.astype(WIRE), 'blk', pairs)]
    all_to_all x2, waiting for transfers between devices: 67 us -> 70.8 us  [routed(): got = lax.all_to_all(x, 'expert', split_axis=0, concat_axis=0, tiled=True)]
  transfers between devices with their start and end apart: 14 -> 14, of which waited for: 7 -> 6; matrix products, arithmetic and copies ran while one was open for 8% -> 8% of each run, Pallas kernels for 11% -> 13%
where the time goes in v4:
time: 178 us; the launch traced here: 177 us
  waiting for transfers between devices  85.4 us (48%)
  starting transfers between devices  39 us (22%)
  Pallas kernels  32.6 us (18%)
  other arithmetic  16.2 us (9%)
  local copies, waits for them, and re-layouts  3.44 us (2%)
    all_to_all x2, waiting for transfers between devices, routed(): got = lax.all_to_all(x, 'expert', split_axis=0, concat_axis=0, tiled=True)  70.8 us
    all_to_all x2, starting transfers between devices, routed(): got = lax.all_to_all(x, 'expert', split_axis=0, concat_axis=0, tiled=True)  19.5 us
    ppermute x12, starting transfers between devices, send(): return lax.ppermute(values.astype(WIRE), 'blk', pairs)  19.5 us
    pallas_call x8, Pallas kernels, partial_grams(): pl.pallas_call(kernel, out_shape=shapes, in_specs=[smem] + [vmem] * len(a...  18.9 us
    ppermute x12, waiting for transfers between devices, send(): return lax.ppermute(values.astype(WIRE), 'blk', pairs)  14.5 us
    pallas_call x2, Pallas kernels, pack(): pl.pallas_call(functools.partial(pack_kernel, marked, start), out_shape=j...  10.8 us
    convert_element_type x2, other arithmetic, __init__(): self.merge(behind, far[1]).astype(WIRE)  4.06 us
  transfers between devices with their start and end apart: 14, of which 6 were waited for; matrix products, arithmetic and copies ran while one was open for 8% of the time, Pallas kernels for 13%

profile of v4, /device:TPU:8, one launch (start us, length us, event | category | flops | bytes accessed | tf_op | source)
XLA Modules:
  0.0 177.1 jit_solution(10388163827358419670)
XLA Ops:
  0.0 1.3 copy.4.down_ref
  1.3 5.6 %shard_map.28 = bf16[1024,1536]{1,0:T(8,128)(2,1)} custom-call(s32[1,64]{1,0:T(1,128)} %bitcast.47, s32[64,1]{1,0:T(8,128)} %copy.4.down_ref, bf16[512,2048]{1,0:T(8,128)(2,1)} %activations_ref.3), custom_call_target="tpu_custom_call" | custom-call | tf_op jit(solution)/shard_map/pallas_call | solution.py:160
  6.9 12.1 %all-to-all-start = ((bf16[64,16,1536]{2,1,0:T(8,128)(2,1)}), bf16[64,16,1536]{2,1,0:T(8,128)(2,1)S(1)}, u32[]{:S(2)}, u32[]{:S(2)}) async-start(bf16[64,16,1536]{2,1,0:T(8,128)(2,1)} %bitcast.28), calls=%async_computation | async-start | bytes 6291456 | tf_op jit(solution)/shard_map/all_to_all | solution.py:309
  19.1 5.3 %shard_map.29 = bf16[1024,512]{1,0:T(8,128)(2,1)} custom-call(s32[1,64]{1,0:T(1,128)} %bitcast.48, s32[64,1]{1,0:T(8,128)} %copy.4.down_ref, bf16[512,2048]{1,0:T(8,128)(2,1)} %activations_ref.3), custom_call_target="tpu_custom_call" | custom-call | tf_op jit(solution)/shard_map/pallas_call | solution.py:160
  24.4 67.0 %all-to-all-done = bf16[64,16,1536]{2,1,0:T(8,128)(2,1)S(1)} async-done(((bf16[64,16,1536]{2,1,0:T(8,128)(2,1)}), bf16[64,16,1536]{2,1,0:T(8,128)(2,1)S(1)}, u32[]{:S(2)}, u32[]{:S(2)}) %all-to-all-start) | async-done | bytes 3145760 | tf_op jit(solution)/shard_map/all_to_all | solution.py:309
  91.5 0.2 fusion
  91.6 2.6 %shard_map.30 = (f32[208,1536]{1,0:T(8,128)S(1)}, f32[208,1536]{1,0:T(8,128)S(1)}, f32[8,128]{1,0:T(8,128)S(1)}) custom-call(s32[2]{0:T(128)S(1)} %pad_add_fusion.1.owners_ref, bf16[1024,128]{1,0:T(8,128)(2,1)S(1)} %get-tuple-element.86.corner_ref, bf16[1024,1536]{1,0:T(8,128)(2,1)S(1)} %get-tuple-element.85.x0_ref), custom_call_target="tpu_custom_call" | custom-call | tf_op jit(solution)/shard_map/pallas_call | solution.py:99
  94.3 0.9 convert_element_type.164
  95.2 1.5 collective-permute-start.2
  96.7 0.9 convert_element_type.165
  97.6 1.8 collective-permute-start.3
  99.3 7.4 %all-to-all-start.1 = ((bf16[64,16,512]{2,1,0:T(8,128)(2,1)}), bf16[64,16,512]{2,1,0:T(8,128)(2,1)}, u32[]{:S(2)}, u32[]{:S(2)}) async-start(bf16[64,16,512]{2,1,0:T(8,128)(2,1)} %bitcast.29), calls=%async_computation.1 | async-start | bytes 2097152 | tf_op jit(solution)/shard_map/all_to_all | solution.py:309
  106.8 2.0 %shard_map.31 = (f32[208,1536]{1,0:T(8,128)S(1)}, f32[208,1536]{1,0:T(8,128)S(1)}) custom-call(s32[2]{0:T(128)S(1)} %get-tuple-element.106.owners_ref, f32[8,128]{1,0:T(8,128)S(1)} %get-tuple-element.42.facts_ref.before_ref, bf16[1024,1536]{1,0:T(8,128)(2,1)S(1)} %get-tuple-element.85.x0_ref), custom_call_target="tpu_custom_call" | custom-call | tf_op jit(solution)/shard_map/pallas_call | solution.py:99
  108.8 0.9 convert_element_type.162
  109.8 0.3 collective-permute-start
  110.0 0.9 convert_element_type.163
  111.0 3.0 %collective-permute-start.1 = (f16[208,1536]{1,0:T(8,128)(2,1)}, f16[208,1536]{1,0:T(8,128)(2,1)}, u32[]{:S(2)}, u32[]{:S(2)}) collective-permute-start(f16[208,1536]{1,0:T(8,128)(2,1)} %convert_element_type.163), channel_id=1, source_target_pairs={{0,3},{1,0},{2,1},{3,2},{4,7},{5,4},{6,5},{7,6},{8,11},{9,8},{10,9... | collective-permute-start | bytes 1916936 | tf_op jit(solution)/shard_map/ppermute | solution.py:259
  113.9 1.2 collective-permute-done.3
  115.2 2.0 %shard_map.32 = (f32[208,1536]{1,0:T(8,128)S(1)}, f32[208,1536]{1,0:T(8,128)S(1)}) custom-call(s32[2]{0:T(128)S(1)} %get-tuple-element.107.owners_ref, f32[8,128]{1,0:T(8,128)S(1)} %get-tuple-element.42.facts_ref.before_ref, bf16[1024,1536]{1,0:T(8,128)(2,1)S(1)} %get-tuple-element.85.x0_ref), custom_call_target="tpu_custom_call" | custom-call | tf_op jit(solution)/shard_map/pallas_call | solution.py:99
  117.2 1.0 select_reduce_fusion.1
  118.1 1.0 select_reduce_fusion.3
  119.1 3.4 %select_convert_fusion = (f16[208,1536]{1,0:T(8,128)(2,1)}, f16[208,1536]{1,0:T(8,128)(2,1)}) fusion(f16[208,1536]{1,0:T(8,128)(2,1)} %collective-permute-done.3, f32[208,1536]{1,0:T(8,128)S(1)} %get-tuple-element.45, f32[1536]{0:T(1024)S(1)} %get-tuple-element.71, f32[1536]{0:T(1024)S(1)} %get-tuple-element.68, f32[1536]{0:T(1024)S(1)} %get-tuple-element.67, ...), kind=kLoop, calls=%fused_computation | loop fusion | flops 5111808 | bytes 5173872 | tf_op jit(solution)/shard_map/convert_element_type | solution.py:253
  122.5 1.5 collective-permute-start.8
  124.0 1.8 %collective-permute-start.9 = (f16[208,1536]{1,0:T(8,128)(2,1)}, f16[208,1536]{1,0:T(8,128)(2,1)}, u32[]{:S(2)}, u32[]{:S(2)}) collective-permute-start(f16[208,1536]{1,0:T(8,128)(2,1)} %get-tuple-element.104), channel_id=1, source_target_pairs={{0,3},{1,0},{2,1},{3,2},{4,7},{5,4},{6,5},{7,6},{8,11},{9,8},{10,9... | collective-permute-start | bytes 1916936 | tf_op jit(solution)/shard_map/ppermute | solution.py:259
  125.8 2.0 %shard_map.37 = (f32[208,1536]{1,0:T(8,128)S(1)}, f32[208,1536]{1,0:T(8,128)S(1)}) custom-call(s32[2]{0:T(128)S(1)} %pad_add_fusion.owners_ref, f32[8,128]{1,0:T(8,128)S(1)} %get-tuple-element.42.facts_ref.before_ref, bf16[1024,1536]{1,0:T(8,128)(2,1)S(1)} %get-tuple-element.85.x0_ref), custom_call_target="tpu_custom_call" | custom-call | tf_op jit(solution)/shard_map/pallas_call | solution.py:99
  127.8 1.0 copy-done
  128.9 1.0 copy-done.2
  129.9 3.8 %all-to-all-done.1 = bf16[64,16,512]{2,1,0:T(8,128)(2,1)} async-done(((bf16[64,16,512]{2,1,0:T(8,128)(2,1)}), bf16[64,16,512]{2,1,0:T(8,128)(2,1)}, u32[]{:S(2)}, u32[]{:S(2)}) %all-to-all-start.1) | async-done | bytes 1048608 | tf_op jit(solution)/shard_map/all_to_all | solution.py:309
  133.8 2.6 %shard_map.33 = (f32[464,512]{1,0:T(8,128)S(1)}, f32[464,512]{1,0:T(8,128)S(1)}, f32[8,128]{1,0:T(8,128)S(1)}) custom-call(s32[2]{0:T(128)S(1)} %pad_add_fusion.1.owners_ref, f32[8,128]{1,0:T(8,128)S(1)} %get-tuple-element.42.facts_ref.before_ref, bf16[1024,1536]{1,0:T(8,128)(2,1)S(1)} %get-tuple-element.85.x0_ref, bf16[1024,512]{1,0:T(8,128)(2,1)} %bitcast.8.x1_ref), custom_call_target="tpu_custom_call" | custom-call | tf_op jit(solution)/shard_map/pallas_call | solution.py:99
  136.4 0.1 convert_element_type.176
  136.5 0.4 collective-permute-start.4
  137.0 3.0 %collective-permute-start.5 = (f16[464,512]{1,0:T(8,128)(2,1)S(1)}, f16[464,512]{1,0:T(8,128)(2,1)S(1)}, u32[]{:S(2)}, u32[]{:S(2)}) collective-permute-start(f16[464,512]{1,0:T(8,128)(2,1)S(1)} %convert_element_type.177), channel_id=1, source_target_pairs={{0,3},{1,0},{2,1},{3,2},{4,7},{5,4},{6,5},{7,6},{8,11},{9,8},{10,9... | collective-permute-start | bytes 1425416 | tf_op jit(solution)/shard_map/ppermute | solution.py:259
  140.0 2.6 %shard_map.34 = (f32[464,512]{1,0:T(8,128)S(1)}, f32[464,512]{1,0:T(8,128)S(1)}) custom-call(s32[2]{0:T(128)S(1)} %get-tuple-element.106.owners_ref, f32[8,128]{1,0:T(8,128)S(1)} %get-tuple-element.54.facts_ref, bf16[1024,1536]{1,0:T(8,128)(2,1)S(1)} %get-tuple-element.85.x0_ref, bf16[1024,512]{1,0:T(8,128)(2,1)} %bitcast.8.x1_ref), custom_call_target="tpu_custom_call" | custom-call | tf_op jit(solution)/shard_map/pallas_call | solution.py:99
  142.9 3.2 %collective-permute-start.7 = (f16[464,512]{1,0:T(8,128)(2,1)S(1)}, f16[464,512]{1,0:T(8,128)(2,1)S(1)}, u32[]{:S(2)}, u32[]{:S(2)}) collective-permute-start(f16[464,512]{1,0:T(8,128)(2,1)S(1)} %convert_element_type.179), channel_id=1, source_target_pairs={{0,3},{1,0},{2,1},{3,2},{4,7},{5,4},{6,5},{7,6},{8,11},{9,8},{10,9... | collective-permute-start | bytes 1425416 | tf_op jit(solution)/shard_map/ppermute | solution.py:259
  146.1 0.8 multiply_reduce_fusion.4
  146.9 0.8 multiply_reduce_fusion.5
  147.8 1.0 multiply_reduce_fusion.3
  148.8 2.3 %add_multiply_fusion = (f32[192,1536]{1,0:T(8,128)S(1)}, f32[192,1536]{1,0:T(8,128)S(1)}) fusion(f32[208,1536]{1,0:T(8,128)S(1)} %copy-done.1, f32[1536]{0:T(1024)S(1)} %get-tuple-element.95, f16[208,1536]{1,0:T(8,128)(2,1)} %collective-permute-done.9, f32[1536]{0:T(1024)S(1)} %get-tuple-element.94, f16[208,1536]{1,0:T(8,128)(2,1)} %collective-permute-done, ...), kind=kLoop, calls=%fused_computation.2 | loop fusion | flops 4718592 | bytes 7120896 | tf_op jit(solution)/shard_map/mul | solution.py:348
  151.1 1.5 shard_map.38.before_ref
  152.7 2.5 %shard_map.36 = (f32[464,512]{1,0:T(8,128)S(1)}, f32[464,512]{1,0:T(8,128)S(1)}) custom-call(s32[2]{0:T(128)S(1)} %get-tuple-element.107.owners_ref, f32[8,128]{1,0:T(8,128)S(1)} %get-tuple-element.54.facts_ref, bf16[1024,1536]{1,0:T(8,128)(2,1)S(1)} %get-tuple-element.85.x0_ref, bf16[1024,512]{1,0:T(8,128)(2,1)} %bitcast.8.x1_ref), custom_call_target="tpu_custom_call" | custom-call | tf_op jit(solution)/shard_map/pallas_call | solution.py:99
  155.3 0.7 select_convert_fusion.2
  156.0 2.5 %shard_map.35 = (f32[464,512]{1,0:T(8,128)S(1)}, f32[464,512]{1,0:T(8,128)S(1)}) custom-call(s32[2]{0:T(128)S(1)} %pad_add_fusion.owners_ref, f32[8,128]{1,0:T(8,128)S(1)} %get-tuple-element.54.facts_ref, bf16[1024,1536]{1,0:T(8,128)(2,1)S(1)} %get-tuple-element.85.x0_ref, bf16[1024,512]{1,0:T(8,128)(2,1)} %bitcast.8.x1_ref), custom_call_target="tpu_custom_call" | custom-call | tf_op jit(solution)/shard_map/pallas_call | solution.py:99
  158.6 3.1 %collective-permute-start.11 = (f16[464,512]{1,0:T(8,128)(2,1)S(1)}, f16[464,512]{1,0:T(8,128)(2,1)S(1)}, u32[]{:S(2)}, u32[]{:S(2)}) collective-permute-start(f16[464,512]{1,0:T(8,128)(2,1)S(1)} %get-tuple-element.102), channel_id=1, source_target_pairs={{0,3},{1,0},{2,1},{3,2},{4,7},{5,4},{6,5},{7,6},{8,11},{9,8},{10,9... | collective-permute-start | bytes 1425416 | tf_op jit(solution)/shard_map/ppermute | solution.py:259
  161.7 1.1 collective-permute-done.7
  162.8 10.0 %collective-permute-done.11 = f16[464,512]{1,0:T(8,128)(2,1)S(1)} collective-permute-done((f16[464,512]{1,0:T(8,128)(2,1)S(1)}, f16[464,512]{1,0:T(8,128)(2,1)S(1)}, u32[]{:S(2)}, u32[]{:S(2)}) %collective-permute-start.11) | collective-permute-done | bytes 475168 | tf_op jit(solution)/shard_map/ppermute | solution.py:259
  172.8 2.2 %collective-permute-done.6 = f16[464,512]{1,0:T(8,128)(2,1)S(1)} collective-permute-done((f16[464,512]{1,0:T(8,128)(2,1)S(1)}, f16[464,512]{1,0:T(8,128)(2,1)S(1)}, u32[]{:S(2)}, u32[]{:S(2)}) %collective-permute-start.6) | collective-permute-done | bytes 475168 | tf_op jit(solution)/shard_map/ppermute | solution.py:259
  175.0 0.6 add_multiply_fusion.2
  175.6 1.4 shard_map.39
  (39 shorter events, 0.8 us)
Async XLA Ops:
  6.9 84.5 %all-to-all-start = ((bf16[64,16,1536]{2,1,0:T(8,128)(2,1)}), bf16[64,16,1536]{2,1,0:T(8,128)(2,1)S(1)}, u32[]{:S(2)}, u32[]{:S(2)}) async-start(bf16[64,16,1536]{2,1,0:T(8,128)(2,1)} %bitcast.28), calls=%async_computation | async-start | bytes 6291456 | tf_op jit(solution)/shard_map/all_to_all | solution.py:309
  95.2 18.7 %collective-permute-start.2 = (f16[208,1536]{1,0:T(8,128)(2,1)}, f16[208,1536]{1,0:T(8,128)(2,1)}, u32[]{:S(2)}, u32[]{:S(2)}) collective-permute-start(f16[208,1536]{1,0:T(8,128)(2,1)} %convert_element_type.164), channel_id=1, source_target_pairs={{0,1},{1,2},{2,3},{3,0},{4,5},{5,6},{6,7},{7,4},{8,9},{9,10},{10,1... | collective-permute-start | bytes 1916936 | tf_op jit(solution)/shard_map/ppermute | solution.py:259
  97.6 17.6 %collective-permute-start.3 = (f16[208,1536]{1,0:T(8,128)(2,1)}, f16[208,1536]{1,0:T(8,128)(2,1)}, u32[]{:S(2)}, u32[]{:S(2)}) collective-permute-start(f16[208,1536]{1,0:T(8,128)(2,1)} %convert_element_type.165), channel_id=1, source_target_pairs={{0,3},{1,0},{2,1},{3,2},{4,7},{5,4},{6,5},{7,6},{8,11},{9,8},{10,9... | collective-permute-start | bytes 1916936 | tf_op jit(solution)/shard_map/ppermute | solution.py:259
  99.3 34.4 %all-to-all-start.1 = ((bf16[64,16,512]{2,1,0:T(8,128)(2,1)}), bf16[64,16,512]{2,1,0:T(8,128)(2,1)}, u32[]{:S(2)}, u32[]{:S(2)}) async-start(bf16[64,16,512]{2,1,0:T(8,128)(2,1)} %bitcast.29), calls=%async_computation.1 | async-start | bytes 2097152 | tf_op jit(solution)/shard_map/all_to_all | solution.py:309
  109.8 20.2 %collective-permute-start = (f16[208,1536]{1,0:T(8,128)(2,1)}, f16[208,1536]{1,0:T(8,128)(2,1)}, u32[]{:S(2)}, u32[]{:S(2)}) collective-permute-start(f16[208,1536]{1,0:T(8,128)(2,1)} %convert_element_type.162), channel_id=1, source_target_pairs={{0,1},{1,2},{2,3},{3,0},{4,5},{5,6},{6,7},{7,4},{8,9},{9,10},{10,1... | collective-permute-start | bytes 1916936 | tf_op jit(solution)/shard_map/ppermute | solution.py:259
  111.0 19.0 %collective-permute-start.1 = (f16[208,1536]{1,0:T(8,128)(2,1)}, f16[208,1536]{1,0:T(8,128)(2,1)}, u32[]{:S(2)}, u32[]{:S(2)}) collective-permute-start(f16[208,1536]{1,0:T(8,128)(2,1)} %convert_element_type.163), channel_id=1, source_target_pairs={{0,3},{1,0},{2,1},{3,2},{4,7},{5,4},{6,5},{7,6},{8,11},{9,8},{10,9... | collective-permute-start | bytes 1916936 | tf_op jit(solution)/shard_map/ppermute | solution.py:259
  122.5 20.4 %collective-permute-start.8 = (f16[208,1536]{1,0:T(8,128)(2,1)}, f16[208,1536]{1,0:T(8,128)(2,1)}, u32[]{:S(2)}, u32[]{:S(2)}) collective-permute-start(f16[208,1536]{1,0:T(8,128)(2,1)} %get-tuple-element.105), channel_id=1, source_target_pairs={{0,1},{1,2},{2,3},{3,0},{4,5},{5,6},{6,7},{7,4},{8,9},{9,10},{10,1... | collective-permute-start | bytes 1916936 | tf_op jit(solution)/shard_map/ppermute | solution.py:259
  124.0 18.9 %collective-permute-start.9 = (f16[208,1536]{1,0:T(8,128)(2,1)}, f16[208,1536]{1,0:T(8,128)(2,1)}, u32[]{:S(2)}, u32[]{:S(2)}) collective-permute-start(f16[208,1536]{1,0:T(8,128)(2,1)} %get-tuple-element.104), channel_id=1, source_target_pairs={{0,3},{1,0},{2,1},{3,2},{4,7},{5,4},{6,5},{7,6},{8,11},{9,8},{10,9... | collective-permute-start | bytes 1916936 | tf_op jit(solution)/shard_map/ppermute | solution.py:259
  127.8 1.0 copy-start
  128.9 1.0 copy-start.2
  136.5 16.1 %collective-permute-start.4 = (f16[464,512]{1,0:T(8,128)(2,1)S(1)}, f16[464,512]{1,0:T(8,128)(2,1)S(1)}, u32[]{:S(2)}, u32[]{:S(2)}) collective-permute-start(f16[464,512]{1,0:T(8,128)(2,1)S(1)} %convert_element_type.176), channel_id=1, source_target_pairs={{0,1},{1,2},{2,3},{3,0},{4,5},{5,6},{6,7},{7,4},{8,9},{9,10},{10,1... | collective-permute-start | bytes 1425416 | tf_op jit(solution)/shard_map/ppermute | solution.py:259
  137.0 15.7 %collective-permute-start.5 = (f16[464,512]{1,0:T(8,128)(2,1)S(1)}, f16[464,512]{1,0:T(8,128)(2,1)S(1)}, u32[]{:S(2)}, u32[]{:S(2)}) collective-permute-start(f16[464,512]{1,0:T(8,128)(2,1)S(1)} %convert_element_type.177), channel_id=1, source_target_pairs={{0,3},{1,0},{2,1},{3,2},{4,7},{5,4},{6,5},{7,6},{8,11},{9,8},{10,9... | collective-permute-start | bytes 1425416 | tf_op jit(solution)/shard_map/ppermute | solution.py:259
  142.6 5.2 %copy-start.1 = (f32[208,1536]{1,0:T(8,128)S(1)}, f32[208,1536]{1,0:T(8,128)}, u32[]{:S(2)}) copy-start(f32[208,1536]{1,0:T(8,128)} %copy-done) | copy-start | bytes 3833860
  142.6 6.2 %copy-start.3 = (f32[208,1536]{1,0:T(8,128)S(1)}, f32[208,1536]{1,0:T(8,128)}, u32[]{:S(2)}) copy-start(f32[208,1536]{1,0:T(8,128)} %copy-done.2) | copy-start | bytes 3833860
  142.8 18.9 %collective-permute-start.10 = (f16[464,512]{1,0:T(8,128)(2,1)S(1)}, f16[464,512]{1,0:T(8,128)(2,1)S(1)}, u32[]{:S(2)}, u32[]{:S(2)}) collective-permute-start(f16[464,512]{1,0:T(8,128)(2,1)S(1)} %convert_element_type.178), channel_id=1, source_target_pairs={{0,1},{1,2},{2,3},{3,0},{4,5},{5,6},{6,7},{7,4},{8,9},{9,10},{10,1... | collective-permute-start | bytes 1425416 | tf_op jit(solution)/shard_map/ppermute | solution.py:259
  142.9 19.9 %collective-permute-start.7 = (f16[464,512]{1,0:T(8,128)(2,1)S(1)}, f16[464,512]{1,0:T(8,128)(2,1)S(1)}, u32[]{:S(2)}, u32[]{:S(2)}) collective-permute-start(f16[464,512]{1,0:T(8,128)(2,1)S(1)} %convert_element_type.179), channel_id=1, source_target_pairs={{0,3},{1,0},{2,1},{3,2},{4,7},{5,4},{6,5},{7,6},{8,11},{9,8},{10,9... | collective-permute-start | bytes 1425416 | tf_op jit(solution)/shard_map/ppermute | solution.py:259
  158.6 14.2 %collective-permute-start.11 = (f16[464,512]{1,0:T(8,128)(2,1)S(1)}, f16[464,512]{1,0:T(8,128)(2,1)S(1)}, u32[]{:S(2)}, u32[]{:S(2)}) collective-permute-start(f16[464,512]{1,0:T(8,128)(2,1)S(1)} %get-tuple-element.102), channel_id=1, source_target_pairs={{0,3},{1,0},{2,1},{3,2},{4,7},{5,4},{6,5},{7,6},{8,11},{9,8},{10,9... | collective-permute-start | bytes 1425416 | tf_op jit(solution)/shard_map/ppermute | solution.py:259
  161.6 13.4 %collective-permute-start.6 = (f16[464,512]{1,0:T(8,128)(2,1)S(1)}, f16[464,512]{1,0:T(8,128)(2,1)S(1)}, u32[]{:S(2)}, u32[]{:S(2)}) collective-permute-start(f16[464,512]{1,0:T(8,128)(2,1)S(1)} %get-tuple-element.103), channel_id=1, source_target_pairs={{0,1},{1,2},{2,3},{3,0},{4,5},{5,6},{6,7},{7,4},{8,9},{9,10},{10,1... | collective-permute-start | bytes 1425416 | tf_op jit(solution)/shard_map/ppermute | solution.py:259

commit v5 on v4

--- a/solution.py
+++ b/solution.py
@@ -55,11 +55,19 @@
     half = first // 2
     scale = scale_and_notes(facts_ref, upper_ref, lower_ref)
     for h, ref in enumerate((upper_ref, lower_ref)):
-        left = x0_ref[:, pl.ds(pl.multiple_of(owners_ref[h] * first, 128), first)]
-        left = left[:, h * half : (h + 1) * half]
-        for j in range(x0_ref.shape[1] // 512):
-            block = rows_dot(left, x0_ref[:, 512 * j : 512 * (j + 1)])
-            ref[:half, 512 * j : 512 * (j + 1)] = block * scale
+        own = x0_ref[:, pl.ds(pl.multiple_of(owners_ref[h] * first, 128), first)]
+        if h == 0:
+            ref[:128, :256] = rows_dot(own[:, :128], own[:, :256]) * scale
+            ref[128:half, :256] = rows_dot(own[:, 128:half], own[:, 128:]) * scale
+        else:
+            ref[:64, :256] = rows_dot(own[:, half:256], own[:, 128:]) * scale
+            ref[64:half, :128] = rows_dot(own[:, 256:], own[:, 256:]) * scale
+            ref[64:half, 128:256] = rows_dot(own[:, 256:], own[:, :128]) * scale
+        left = own[:, h * half : (h + 1) * half]
+        for r in range(1, 4):
+            other = pl.multiple_of(lax.rem(owners_ref[h] + r, 4) * first, 128)
+            block = rows_dot(left, x0_ref[:, pl.ds(other, first)])
+            ref[:half, 256 + first * (r - 1) : 256 + first * r] = block * scale
 
 
 def second_body(owners_ref, facts_ref, x0_ref, x1_ref, upper_ref, lower_ref):
@@ -102,7 +110,9 @@
         in_specs=[smem] + [vmem] * len(arrays),
         out_specs=[vmem] * len(shapes),
         compiler_params=pltpu.CompilerParams(vmem_limit_bytes=40 * 1024 * 1024),
-        cost_estimate=pl.CostEstimate(flops=0, bytes_accessed=0, transcendentals=0),
+        cost_estimate=pl.CostEstimate(
+            flops=2000000000 if kernel is first_body else 0, bytes_accessed=0, transcendentals=0
+        ),
     )(owners, *arrays)
 
 
@@ -182,20 +192,26 @@
         copy.wait()
 
 
-def place_first(upper_ref, lower_ref, out_ref, sem):
-    half, first = upper_ref.shape[0], upper_ref.shape[1] // 4
-    strip = out_ref.shape[1] // 4
-    copies(
-        [
-            (
-                ref.at[:, d * first : (d + 1) * first],
-                out_ref.at[h * half : (h + 1) * half, d * strip : d * strip + first],
-            )
-            for h, ref in enumerate((upper_ref, lower_ref))
-            for d in range(4)
-        ],
-        sem,
-    )
+def place_first(me_ref, upper_ref, lower_ref, out_ref, square_ref, sem):
+    half = upper_ref.shape[0]
+    first, strip = 2 * half, out_ref.shape[1] // 4
+    square_ref[:128, :256] = upper_ref[:128, :256]
+    square_ref[128:half, 128:] = upper_ref[128:, :256]
+    square_ref[half:256, 128:] = lower_ref[:64, :256]
+    square_ref[256:, 256:] = lower_ref[64:, :128]
+    square_ref[256:, :128] = lower_ref[64:, 128:256]
+    square_ref[128:256, :128] = square_ref[:128, 128:256].T
+    square_ref[256:, 128:256] = square_ref[128:256, 256:].T
+    square_ref[:128, 256:] = square_ref[256:, :128].T
+    column = pl.multiple_of(me_ref[0] * strip, 128)
+    pieces = [(square_ref, out_ref.at[:first, pl.ds(column, first)])]
+    for r in range(1, 4):
+        column = pl.multiple_of(lax.rem(me_ref[0] + r, 4) * strip, 128)
+        for h, ref in enumerate((upper_ref, lower_ref)):
+            source = ref.at[:, 256 + first * (r - 1) : 256 + first * r]
+            rows = slice(h * half, (h + 1) * half)
+            pieces.append((source, out_ref.at[rows, pl.ds(column, first)]))
+    copies(pieces, sem)
 
 
 def place_second(upper_ref, lower_ref, before_ref, out_ref, sem):
@@ -217,17 +233,24 @@
     copies(pieces, sem)
 
 
-def place(kernel, shape, upper, lower, *before):
+def place(kernel, shape, upper, lower, me=None, before=None):
     hbm, vmem = pl.BlockSpec(memory_space=pltpu.HBM), pl.BlockSpec(memory_space=pltpu.VMEM)
+    smem = pl.BlockSpec(memory_space=pltpu.SMEM)
+    scratch = [pltpu.SemaphoreType.DMA((16,))]
+    if before is None:
+        specs, arrays = [smem, vmem, vmem], (me.reshape(1), upper, lower)
+        scratch = [pltpu.VMEM((FIRST, FIRST), jnp.float32)] + scratch
+    else:
+        specs, arrays = [vmem, vmem, hbm], (upper, lower, before)
     return pl.pallas_call(
         kernel,
         out_shape=jax.ShapeDtypeStruct(shape, jnp.float32),
-        in_specs=[vmem, vmem] + [hbm] * len(before),
+        in_specs=specs,
         out_specs=hbm,
-        input_output_aliases={2: 0} if before else {},
-        scratch_shapes=[pltpu.SemaphoreType.DMA((16,))],
+        input_output_aliases={} if before is None else {2: 0},
+        scratch_shapes=scratch,
         compiler_params=pltpu.CompilerParams(vmem_limit_bytes=24 * 1024 * 1024),
-    )(upper, lower, *before)
+    )(*arrays)
 
 
 def fourth(value):
@@ -321,12 +344,13 @@
     x0 = lax.dynamic_update_slice(x0, jnp.where(is_mark, jnp.zeros_like(corner), corner), (0, 0))
 
     half0, half1 = FIRST // 2, FIRST + last // 2
+    wide0 = 256 + (ranks - 1) * FIRST
     ring0 = Ring(
         lambda: partial_grams(
-            first_far, half0, ranks * FIRST, owners((2, 2)), corner, x0, facts=True
+            first_far, half0, wide0, owners((2, 2)), corner, x0, facts=True
         ),
         lambda facts, *offsets: partial_grams(
-            first_body, half0, ranks * FIRST, owners(offsets), facts, x0
+            first_body, half0, wide0, owners(offsets), facts, x0
         ),
         ranks,
     )
@@ -345,10 +369,10 @@
     sums0, empty_blocks = ring0.total()
     hessian_scale = 2.0 / (float(ranks * slot_rows) - block_rows * empty_blocks)
     shape = (strip, width)
-    out = place(place_first, shape, *[half * hessian_scale for half in sums0])
+    out = place(place_first, shape, *[half * hessian_scale for half in sums0], me=me)
     sums1, _ = ring1.total()
     hessian_scale = hessian_scale[:, : ranks * last]
-    out = place(place_second, shape, *[half * hessian_scale for half in sums1], out)
+    out = place(place_second, shape, *[half * hessian_scale for half in sums1], before=out)
     return out[None]
 
 

time: 178 us -> 179 us (level)
  other arithmetic: 16.2 us -> 14 us
    mul x2 -> x0, other arithmetic: 3.29 us -> none  [on_device(): out = place(place_first, shape, *[half * hessian_scale for half in sums0])]
    mul x2 -> x4, other arithmetic: 0.56 us -> 3.53 us  [on_device(): half * hessian_scale]
    unnamed x9 -> x13, local copies, waits for them, and re-layouts: 3.44 us -> 4.2 us
  transfers between devices with their start and end apart: 14 -> 14, of which waited for: 6 -> 6; matrix products, arithmetic and copies ran while one was open for 8% -> 7% of each run, Pallas kernels for 13% -> 14%
where the time goes in v5:
time: 179 us; the launch traced here: 178 us
  waiting for transfers between devices  85.8 us (48%)
  starting transfers between devices  38.7 us (22%)
  Pallas kernels  34.3 us (19%)
  other arithmetic  14 us (8%)
  local copies, waits for them, and re-layouts  4.2 us (2%)
    all_to_all x2, waiting for transfers between devices, routed(): got = lax.all_to_all(x, 'expert', split_axis=0, concat_axis=0, tiled=True)  70.5 us
    pallas_call x8, Pallas kernels, partial_grams(): pl.pallas_call(kernel, out_shape=shapes, in_specs=[smem] + [vmem] * len(a...  20.4 us
    all_to_all x2, starting transfers between devices, routed(): got = lax.all_to_all(x, 'expert', split_axis=0, concat_axis=0, tiled=True)  19.5 us
    ppermute x12, starting transfers between devices, send(): return lax.ppermute(values.astype(WIRE), 'blk', pairs)  19.2 us
    ppermute x12, waiting for transfers between devices, send(): return lax.ppermute(values.astype(WIRE), 'blk', pairs)  15.3 us
    pallas_call x2, Pallas kernels, pack(): pl.pallas_call(functools.partial(pack_kernel, marked, start), out_shape=j...  10.9 us
    unnamed x13, local copies, waits for them, and re-layouts  4.2 us
    convert_element_type x2, other arithmetic, __init__(): self.merge(behind, far[1]).astype(WIRE)  4.1 us
  transfers between devices with their start and end apart: 14, of which 6 were waited for; matrix products, arithmetic and copies ran while one was open for 7% of the time, Pallas kernels for 14%

profile of v5, /device:TPU:8, one launch (start us, length us, event | category | flops | bytes accessed | tf_op | source)
XLA Modules:
  0.0 177.6 jit_solution(18358194033641339739)
XLA Ops:
  0.0 1.3 copy.4.down_ref
  1.3 5.6 %shard_map.28 = bf16[1024,1536]{1,0:T(8,128)(2,1)} custom-call(s32[1,64]{1,0:T(1,128)} %bitcast.48, s32[64,1]{1,0:T(8,128)} %copy.4.down_ref, bf16[512,2048]{1,0:T(8,128)(2,1)} %activations_ref.3), custom_call_target="tpu_custom_call" | custom-call | tf_op jit(solution)/shard_map/pallas_call | solution.py:170
  6.9 12.1 %all-to-all-start = ((bf16[64,16,1536]{2,1,0:T(8,128)(2,1)}), bf16[64,16,1536]{2,1,0:T(8,128)(2,1)S(1)}, u32[]{:S(2)}, u32[]{:S(2)}) async-start(bf16[64,16,1536]{2,1,0:T(8,128)(2,1)} %bitcast.29), calls=%async_computation | async-start | bytes 6291456 | tf_op jit(solution)/shard_map/all_to_all | solution.py:332
  19.1 5.3 %shard_map.29 = bf16[1024,512]{1,0:T(8,128)(2,1)} custom-call(s32[1,64]{1,0:T(1,128)} %bitcast.49, s32[64,1]{1,0:T(8,128)} %copy.4.down_ref, bf16[512,2048]{1,0:T(8,128)(2,1)} %activations_ref.3), custom_call_target="tpu_custom_call" | custom-call | tf_op jit(solution)/shard_map/pallas_call | solution.py:170
  24.4 67.0 %all-to-all-done = bf16[64,16,1536]{2,1,0:T(8,128)(2,1)S(1)} async-done(((bf16[64,16,1536]{2,1,0:T(8,128)(2,1)}), bf16[64,16,1536]{2,1,0:T(8,128)(2,1)S(1)}, u32[]{:S(2)}, u32[]{:S(2)}) %all-to-all-start) | async-done | bytes 3145760 | tf_op jit(solution)/shard_map/all_to_all | solution.py:332
  91.5 0.2 fusion
  91.6 3.0 %shard_map.30 = (f32[208,1408]{1,0:T(8,128)S(1)}, f32[208,1408]{1,0:T(8,128)S(1)}, f32[8,128]{1,0:T(8,128)S(1)}) custom-call(s32[2]{0:T(128)S(1)} %pad_add_fusion.1.owners_ref, bf16[1024,128]{1,0:T(8,128)(2,1)S(1)} %get-tuple-element.86.corner_ref, bf16[1024,1536]{1,0:T(8,128)(2,1)S(1)} %get-tuple-element.85.x0_ref), custom_call_target="tpu_custom_call" | custom-call | tf_op jit(solution)/shard_map/pallas_call | solution.py:107
  94.7 0.9 convert_element_type.164
  95.5 1.5 collective-permute-start.2
  97.0 0.9 convert_element_type.165
  97.9 1.7 collective-permute-start.3
  99.7 7.4 %all-to-all-start.1 = ((bf16[64,16,512]{2,1,0:T(8,128)(2,1)}), bf16[64,16,512]{2,1,0:T(8,128)(2,1)}, u32[]{:S(2)}, u32[]{:S(2)}) async-start(bf16[64,16,512]{2,1,0:T(8,128)(2,1)} %bitcast.30), calls=%async_computation.1 | async-start | bytes 2097152 | tf_op jit(solution)/shard_map/all_to_all | solution.py:332
  107.2 2.4 %shard_map.31 = (f32[208,1408]{1,0:T(8,128)S(1)}, f32[208,1408]{1,0:T(8,128)S(1)}) custom-call(s32[2]{0:T(128)S(1)} %get-tuple-element.106.owners_ref, f32[8,128]{1,0:T(8,128)S(1)} %get-tuple-element.42.facts_ref.before_ref, bf16[1024,1536]{1,0:T(8,128)(2,1)S(1)} %get-tuple-element.85.x0_ref), custom_call_target="tpu_custom_call" | custom-call | flops 2000000000 | tf_op jit(solution)/shard_map/pallas_call | solution.py:107
  109.6 0.3 collective-permute-start
  110.0 3.0 %collective-permute-start.1 = (f16[208,1408]{1,0:T(8,128)(2,1)S(1)}, f16[208,1408]{1,0:T(8,128)(2,1)}, u32[]{:S(2)}, u32[]{:S(2)}) collective-permute-start(f16[208,1408]{1,0:T(8,128)(2,1)S(1)} %convert_element_type.163), channel_id=1, source_target_pairs={{0,3},{1,0},{2,1},{3,2},{4,7},{5,4},{6,5},{7,6},{8,11},{9,8},{10,9... | collective-permute-start | bytes 1757192 | tf_op jit(solution)/shard_map/ppermute | solution.py:282
  113.1 1.3 collective-permute-done.3
  114.3 2.4 %shard_map.32 = (f32[208,1408]{1,0:T(8,128)S(1)}, f32[208,1408]{1,0:T(8,128)S(1)}) custom-call(s32[2]{0:T(128)S(1)} %get-tuple-element.107.owners_ref, f32[8,128]{1,0:T(8,128)S(1)} %get-tuple-element.42.facts_ref.before_ref, bf16[1024,1536]{1,0:T(8,128)(2,1)S(1)} %get-tuple-element.85.x0_ref), custom_call_target="tpu_custom_call" | custom-call | flops 2000000000 | tf_op jit(solution)/shard_map/pallas_call | solution.py:107
  116.7 0.9 select_reduce_fusion.1
  117.7 1.0 select_reduce_fusion.3
  118.6 3.4 %select_convert_fusion = (f16[208,1408]{1,0:T(8,128)(2,1)}, f16[208,1408]{1,0:T(8,128)(2,1)}) fusion(f16[208,1408]{1,0:T(8,128)(2,1)} %collective-permute-done.3, f32[208,1408]{1,0:T(8,128)S(1)} %get-tuple-element.45, f32[1408]{0:T(1024)S(1)} %get-tuple-element.71, f32[1408]{0:T(1024)S(1)} %get-tuple-element.68, f32[1408]{0:T(1024)S(1)} %get-tuple-element.67, ...), kind=kLoop, calls=%fused_computation | loop fusion | flops 4685824 | bytes 4742768 | tf_op jit(solution)/shard_map/convert_element_type | solution.py:276
  122.0 1.5 collective-permute-start.8
  123.5 1.8 collective-permute-start.9
  125.3 2.4 %shard_map.37 = (f32[208,1408]{1,0:T(8,128)S(1)}, f32[208,1408]{1,0:T(8,128)S(1)}) custom-call(s32[2]{0:T(128)S(1)} %pad_add_fusion.owners_ref, f32[8,128]{1,0:T(8,128)S(1)} %get-tuple-element.42.facts_ref.before_ref, bf16[1024,1536]{1,0:T(8,128)(2,1)S(1)} %get-tuple-element.85.x0_ref), custom_call_target="tpu_custom_call" | custom-call | flops 2000000000 | tf_op jit(solution)/shard_map/pallas_call | solution.py:107
  127.8 1.0 copy-done
  128.8 1.0 copy-done.2
  129.8 0.8 copy-done.4
  130.6 3.4 %all-to-all-done.1 = bf16[64,16,512]{2,1,0:T(8,128)(2,1)} async-done(((bf16[64,16,512]{2,1,0:T(8,128)(2,1)}), bf16[64,16,512]{2,1,0:T(8,128)(2,1)}, u32[]{:S(2)}, u32[]{:S(2)}) %all-to-all-start.1) | async-done | bytes 1048608 | tf_op jit(solution)/shard_map/all_to_all | solution.py:332
  134.1 2.6 %shard_map.33 = (f32[464,512]{1,0:T(8,128)S(1)}, f32[464,512]{1,0:T(8,128)S(1)}, f32[8,128]{1,0:T(8,128)S(1)}) custom-call(s32[2]{0:T(128)S(1)} %pad_add_fusion.1.owners_ref, f32[8,128]{1,0:T(8,128)S(1)} %get-tuple-element.42.facts_ref.before_ref, bf16[1024,1536]{1,0:T(8,128)(2,1)S(1)} %get-tuple-element.85.x0_ref, bf16[1024,512]{1,0:T(8,128)(2,1)} %bitcast.8.x1_ref), custom_call_target="tpu_custom_call" | custom-call | tf_op jit(solution)/shard_map/pallas_call | solution.py:107
  136.7 0.1 convert_element_type.176
  136.8 0.6 collective-permute-start.4
  137.5 3.0 %collective-permute-start.5 = (f16[464,512]{1,0:T(8,128)(2,1)S(1)}, f16[464,512]{1,0:T(8,128)(2,1)S(1)}, u32[]{:S(2)}, u32[]{:S(2)}) collective-permute-start(f16[464,512]{1,0:T(8,128)(2,1)S(1)} %convert_element_type.177), channel_id=1, source_target_pairs={{0,3},{1,0},{2,1},{3,2},{4,7},{5,4},{6,5},{7,6},{8,11},{9,8},{10,9... | collective-permute-start | bytes 1425416 | tf_op jit(solution)/shard_map/ppermute | solution.py:282
  140.5 2.6 %shard_map.34 = (f32[464,512]{1,0:T(8,128)S(1)}, f32[464,512]{1,0:T(8,128)S(1)}) custom-call(s32[2]{0:T(128)S(1)} %get-tuple-element.106.owners_ref, f32[8,128]{1,0:T(8,128)S(1)} %get-tuple-element.54.facts_ref, bf16[1024,1536]{1,0:T(8,128)(2,1)S(1)} %get-tuple-element.85.x0_ref, bf16[1024,512]{1,0:T(8,128)(2,1)} %bitcast.8.x1_ref), custom_call_target="tpu_custom_call" | custom-call | tf_op jit(solution)/shard_map/pallas_call | solution.py:107
  143.1 0.1 convert_element_type.178
  143.4 3.2 %collective-permute-start.7 = (f16[464,512]{1,0:T(8,128)(2,1)S(1)}, f16[464,512]{1,0:T(8,128)(2,1)S(1)}, u32[]{:S(2)}, u32[]{:S(2)}) collective-permute-start(f16[464,512]{1,0:T(8,128)(2,1)S(1)} %convert_element_type.179), channel_id=1, source_target_pairs={{0,3},{1,0},{2,1},{3,2},{4,7},{5,4},{6,5},{7,6},{8,11},{9,8},{10,9... | collective-permute-start | bytes 1425416 | tf_op jit(solution)/shard_map/ppermute | solution.py:282
  146.6 0.8 multiply_reduce_fusion.4
  147.5 0.8 multiply_reduce_fusion.5
  148.3 0.9 multiply_reduce_fusion.3
  149.3 2.0 %add_multiply_fusion = (f32[192,1408]{1,0:T(8,128)S(1)}, f32[192,1408]{1,0:T(8,128)S(1)}) fusion(f32[208,1408]{1,0:T(8,128)S(1)} %copy-done.1, f32[1408]{0:T(1024)S(1)} %get-tuple-element.95, f16[208,1408]{1,0:T(8,128)(2,1)} %collective-permute-done.9, f32[1408]{0:T(1024)S(1)} %get-tuple-element.94, f16[208,1408]{1,0:T(8,128)(2,1)S(1)} %copy-done.5, ...), kind=kLoop, calls=%fused_computation.2 | loop fusion | flops 4325376 | bytes 6527488 | tf_op jit(solution)/shard_map/mul | solution.py:372
  151.3 1.7 shard_map.38.before_ref
  153.0 2.5 %shard_map.36 = (f32[464,512]{1,0:T(8,128)S(1)}, f32[464,512]{1,0:T(8,128)S(1)}) custom-call(s32[2]{0:T(128)S(1)} %get-tuple-element.107.owners_ref, f32[8,128]{1,0:T(8,128)S(1)} %get-tuple-element.54.facts_ref, bf16[1024,1536]{1,0:T(8,128)(2,1)S(1)} %get-tuple-element.85.x0_ref, bf16[1024,512]{1,0:T(8,128)(2,1)} %bitcast.8.x1_ref), custom_call_target="tpu_custom_call" | custom-call | tf_op jit(solution)/shard_map/pallas_call | solution.py:107
  155.7 0.7 select_convert_fusion.2
  156.4 2.5 %shard_map.35 = (f32[464,512]{1,0:T(8,128)S(1)}, f32[464,512]{1,0:T(8,128)S(1)}) custom-call(s32[2]{0:T(128)S(1)} %pad_add_fusion.owners_ref, f32[8,128]{1,0:T(8,128)S(1)} %get-tuple-element.54.facts_ref, bf16[1024,1536]{1,0:T(8,128)(2,1)S(1)} %get-tuple-element.85.x0_ref, bf16[1024,512]{1,0:T(8,128)(2,1)} %bitcast.8.x1_ref), custom_call_target="tpu_custom_call" | custom-call | tf_op jit(solution)/shard_map/pallas_call | solution.py:107
  158.9 2.4 %collective-permute-start.11 = (f16[464,512]{1,0:T(8,128)(2,1)S(1)}, f16[464,512]{1,0:T(8,128)(2,1)S(1)}, u32[]{:S(2)}, u32[]{:S(2)}) collective-permute-start(f16[464,512]{1,0:T(8,128)(2,1)S(1)} %get-tuple-element.102), channel_id=1, source_target_pairs={{0,3},{1,0},{2,1},{3,2},{4,7},{5,4},{6,5},{7,6},{8,11},{9,8},{10,9... | collective-permute-start | bytes 1425416 | tf_op jit(solution)/shard_map/ppermute | solution.py:282
  161.3 0.6 collective-permute-done.10
  162.0 10.2 %collective-permute-done.11 = f16[464,512]{1,0:T(8,128)(2,1)S(1)} collective-permute-done((f16[464,512]{1,0:T(8,128)(2,1)S(1)}, f16[464,512]{1,0:T(8,128)(2,1)S(1)}, u32[]{:S(2)}, u32[]{:S(2)}) %collective-permute-start.11) | collective-permute-done | bytes 475168 | tf_op jit(solution)/shard_map/ppermute | solution.py:282
  172.2 3.3 %collective-permute-done.6 = f16[464,512]{1,0:T(8,128)(2,1)S(1)} collective-permute-done((f16[464,512]{1,0:T(8,128)(2,1)S(1)}, f16[464,512]{1,0:T(8,128)(2,1)S(1)}, u32[]{:S(2)}, u32[]{:S(2)}) %collective-permute-start.6) | collective-permute-done | bytes 475168 | tf_op jit(solution)/shard_map/ppermute | solution.py:282
  175.5 0.6 add_multiply_fusion.2
  176.0 1.4 shard_map.39
  (43 shorter events, 0.8 us)
Async XLA Ops:
  6.9 84.5 %all-to-all-start = ((bf16[64,16,1536]{2,1,0:T(8,128)(2,1)}), bf16[64,16,1536]{2,1,0:T(8,128)(2,1)S(1)}, u32[]{:S(2)}, u32[]{:S(2)}) async-start(bf16[64,16,1536]{2,1,0:T(8,128)(2,1)} %bitcast.29), calls=%async_computation | async-start | bytes 6291456 | tf_op jit(solution)/shard_map/all_to_all | solution.py:332
  95.5 17.5 %collective-permute-start.2 = (f16[208,1408]{1,0:T(8,128)(2,1)}, f16[208,1408]{1,0:T(8,128)(2,1)}, u32[]{:S(2)}, u32[]{:S(2)}) collective-permute-start(f16[208,1408]{1,0:T(8,128)(2,1)} %convert_element_type.164), channel_id=1, source_target_pairs={{0,1},{1,2},{2,3},{3,0},{4,5},{5,6},{6,7},{7,4},{8,9},{9,10},{10,1... | collective-permute-start | bytes 1757192 | tf_op jit(solution)/shard_map/ppermute | solution.py:282
  97.9 16.4 %collective-permute-start.3 = (f16[208,1408]{1,0:T(8,128)(2,1)}, f16[208,1408]{1,0:T(8,128)(2,1)}, u32[]{:S(2)}, u32[]{:S(2)}) collective-permute-start(f16[208,1408]{1,0:T(8,128)(2,1)} %convert_element_type.165), channel_id=1, source_target_pairs={{0,3},{1,0},{2,1},{3,2},{4,7},{5,4},{6,5},{7,6},{8,11},{9,8},{10,9... | collective-permute-start | bytes 1757192 | tf_op jit(solution)/shard_map/ppermute | solution.py:282
  99.7 34.4 %all-to-all-start.1 = ((bf16[64,16,512]{2,1,0:T(8,128)(2,1)}), bf16[64,16,512]{2,1,0:T(8,128)(2,1)}, u32[]{:S(2)}, u32[]{:S(2)}) async-start(bf16[64,16,512]{2,1,0:T(8,128)(2,1)} %bitcast.30), calls=%async_computation.1 | async-start | bytes 2097152 | tf_op jit(solution)/shard_map/all_to_all | solution.py:332
  109.6 20.2 %collective-permute-start = (f16[208,1408]{1,0:T(8,128)(2,1)S(1)}, f16[208,1408]{1,0:T(8,128)(2,1)S(1)}, u32[]{:S(2)}, u32[]{:S(2)}) collective-permute-start(f16[208,1408]{1,0:T(8,128)(2,1)S(1)} %convert_element_type.162), channel_id=1, source_target_pairs={{0,1},{1,2},{2,3},{3,0},{4,5},{5,6},{6,7},{7,4},{8,9},{9,10},{10,1... | collective-permute-start | bytes 1757192 | tf_op jit(solution)/shard_map/ppermute | solution.py:282
  110.0 20.6 %collective-permute-start.1 = (f16[208,1408]{1,0:T(8,128)(2,1)S(1)}, f16[208,1408]{1,0:T(8,128)(2,1)}, u32[]{:S(2)}, u32[]{:S(2)}) collective-permute-start(f16[208,1408]{1,0:T(8,128)(2,1)S(1)} %convert_element_type.163), channel_id=1, source_target_pairs={{0,3},{1,0},{2,1},{3,2},{4,7},{5,4},{6,5},{7,6},{8,11},{9,8},{10,9... | collective-permute-start | bytes 1757192 | tf_op jit(solution)/shard_map/ppermute | solution.py:282
  122.0 21.4 %collective-permute-start.8 = (f16[208,1408]{1,0:T(8,128)(2,1)}, f16[208,1408]{1,0:T(8,128)(2,1)}, u32[]{:S(2)}, u32[]{:S(2)}) collective-permute-start(f16[208,1408]{1,0:T(8,128)(2,1)} %get-tuple-element.105), channel_id=1, source_target_pairs={{0,1},{1,2},{2,3},{3,0},{4,5},{5,6},{6,7},{7,4},{8,9},{9,10},{10,1... | collective-permute-start | bytes 1757192 | tf_op jit(solution)/shard_map/ppermute | solution.py:282
  123.5 19.9 %collective-permute-start.9 = (f16[208,1408]{1,0:T(8,128)(2,1)}, f16[208,1408]{1,0:T(8,128)(2,1)}, u32[]{:S(2)}, u32[]{:S(2)}) collective-permute-start(f16[208,1408]{1,0:T(8,128)(2,1)} %get-tuple-element.104), channel_id=1, source_target_pairs={{0,3},{1,0},{2,1},{3,2},{4,7},{5,4},{6,5},{7,6},{8,11},{9,8},{10,9... | collective-permute-start | bytes 1757192 | tf_op jit(solution)/shard_map/ppermute | solution.py:282
  127.7 1.0 copy-start
  128.8 1.0 copy-start.2
  129.8 0.8 copy-start.4
  136.8 16.2 %collective-permute-start.4 = (f16[464,512]{1,0:T(8,128)(2,1)S(1)}, f16[464,512]{1,0:T(8,128)(2,1)S(1)}, u32[]{:S(2)}, u32[]{:S(2)}) collective-permute-start(f16[464,512]{1,0:T(8,128)(2,1)S(1)} %convert_element_type.176), channel_id=1, source_target_pairs={{0,1},{1,2},{2,3},{3,0},{4,5},{5,6},{6,7},{7,4},{8,9},{9,10},{10,1... | collective-permute-start | bytes 1425416 | tf_op jit(solution)/shard_map/ppermute | solution.py:282
  137.5 15.5 %collective-permute-start.5 = (f16[464,512]{1,0:T(8,128)(2,1)S(1)}, f16[464,512]{1,0:T(8,128)(2,1)S(1)}, u32[]{:S(2)}, u32[]{:S(2)}) collective-permute-start(f16[464,512]{1,0:T(8,128)(2,1)S(1)} %convert_element_type.177), channel_id=1, source_target_pairs={{0,3},{1,0},{2,1},{3,2},{4,7},{5,4},{6,5},{7,6},{8,11},{9,8},{10,9... | collective-permute-start | bytes 1425416 | tf_op jit(solution)/shard_map/ppermute | solution.py:282
  143.1 5.2 %copy-start.5 = (f16[208,1408]{1,0:T(8,128)(2,1)S(1)}, f16[208,1408]{1,0:T(8,128)(2,1)}, u32[]{:S(2)}) copy-start(f16[208,1408]{1,0:T(8,128)(2,1)} %copy-done.4) | copy-start | bytes 1757188
  143.1 5.2 %copy-start.1 = (f32[208,1408]{1,0:T(8,128)S(1)}, f32[208,1408]{1,0:T(8,128)}, u32[]{:S(2)}) copy-start(f32[208,1408]{1,0:T(8,128)} %copy-done) | copy-start | bytes 3514372
  143.1 6.2 %copy-start.3 = (f32[208,1408]{1,0:T(8,128)S(1)}, f32[208,1408]{1,0:T(8,128)}, u32[]{:S(2)}) copy-start(f32[208,1408]{1,0:T(8,128)} %copy-done.2) | copy-start | bytes 3514372
  143.3 18.6 %collective-permute-start.10 = (f16[464,512]{1,0:T(8,128)(2,1)S(1)}, f16[464,512]{1,0:T(8,128)(2,1)S(1)}, u32[]{:S(2)}, u32[]{:S(2)}) collective-permute-start(f16[464,512]{1,0:T(8,128)(2,1)S(1)} %convert_element_type.178), channel_id=1, source_target_pairs={{0,1},{1,2},{2,3},{3,0},{4,5},{5,6},{6,7},{7,4},{8,9},{9,10},{10,1... | collective-permute-start | bytes 1425416 | tf_op jit(solution)/shard_map/ppermute | solution.py:282
  143.4 18.5 %collective-permute-start.7 = (f16[464,512]{1,0:T(8,128)(2,1)S(1)}, f16[464,512]{1,0:T(8,128)(2,1)S(1)}, u32[]{:S(2)}, u32[]{:S(2)}) collective-permute-start(f16[464,512]{1,0:T(8,128)(2,1)S(1)} %convert_element_type.179), channel_id=1, source_target_pairs={{0,3},{1,0},{2,1},{3,2},{4,7},{5,4},{6,5},{7,6},{8,11},{9,8},{10,9... | collective-permute-start | bytes 1425416 | tf_op jit(solution)/shard_map/ppermute | solution.py:282
  158.9 13.2 %collective-permute-start.11 = (f16[464,512]{1,0:T(8,128)(2,1)S(1)}, f16[464,512]{1,0:T(8,128)(2,1)S(1)}, u32[]{:S(2)}, u32[]{:S(2)}) collective-permute-start(f16[464,512]{1,0:T(8,128)(2,1)S(1)} %get-tuple-element.102), channel_id=1, source_target_pairs={{0,3},{1,0},{2,1},{3,2},{4,7},{5,4},{6,5},{7,6},{8,11},{9,8},{10,9... | collective-permute-start | bytes 1425416 | tf_op jit(solution)/shard_map/ppermute | solution.py:282
  161.3 14.1 %collective-permute-start.6 = (f16[464,512]{1,0:T(8,128)(2,1)S(1)}, f16[464,512]{1,0:T(8,128)(2,1)S(1)}, u32[]{:S(2)}, u32[]{:S(2)}) collective-permute-start(f16[464,512]{1,0:T(8,128)(2,1)S(1)} %get-tuple-element.103), channel_id=1, source_target_pairs={{0,1},{1,2},{2,3},{3,0},{4,5},{5,6},{6,7},{7,4},{8,9},{9,10},{10,1... | collective-permute-start | bytes 1425416 | tf_op jit(solution)/shard_map/ppermute | solution.py:282
